TPU v7x, 32 devices: a whole 2x2x4 slice. The times are simulated.
32 devices in a mesh: dp: 16 (over z, x, core), blk: 2 (over y).
Axes of the slice: x: 2, y: 2, z: 4, core: 2. Of those that a mesh axis runs over, the one named last changes fastest.
Arguments:
- hidden: bfloat16 [8192, 768], P(('dp', 'blk')), may hold values from -6 to 6
- doc_lengths: int32 [16, 4], P('dp'), may hold values from 1 to 384, 512 in all within a row
- student_first_gain: float32 [768], replicated, may hold values from 0.5 to 1.5
- student_first_shift: float32 [768], replicated, may hold values from -1.25 to 1.25
- student_project_in: bfloat16 [768, 2304], replicated, may hold values from -0.21875 to 0.21875
- student_query_value_bias: float32 [1536], replicated, may hold values from -1.25 to 1.25
- student_attend_out: bfloat16 [768, 768], replicated, may hold values from -1.25 to 1.25
- student_attend_bias: float32 [768], replicated, may hold values from -1.25 to 1.25
- student_second_gain: float32 [768], replicated, may hold values from 0.5 to 1.5
- student_second_shift: float32 [768], replicated, may hold values from -1.25 to 1.25
- student_expand_weight: bfloat16 [768, 3072], replicated, may hold values from -0.21875 to 0.21875
- student_expand_bias: float32 [3072], replicated, may hold values from -1.25 to 1.25
- student_contract_weight: bfloat16 [3072, 768], replicated, may hold values from -0.109375 to 0.109375
- student_contract_bias: float32 [768], replicated, may hold values from -1.25 to 1.25
- teacher_first_gain: float32 [768], replicated, may hold values from 0.5 to 1.5
- teacher_first_shift: float32 [768], replicated, may hold values from -1.25 to 1.25
- teacher_project_in: bfloat16 [768, 2304], replicated, may hold values from -0.21875 to 0.21875
- teacher_query_value_bias: float32 [1536], replicated, may hold values from -1.25 to 1.25
- teacher_attend_out: bfloat16 [768, 768], replicated, may hold values from -1.25 to 1.25
- teacher_attend_bias: float32 [768], replicated, may hold values from -1.25 to 1.25
- teacher_second_gain: float32 [768], replicated, may hold values from 0.5 to 1.5
- teacher_second_shift: float32 [768], replicated, may hold values from -1.25 to 1.25
- teacher_expand_weight: bfloat16 [768, 3072], replicated, may hold values from -0.21875 to 0.21875
- teacher_expand_bias: float32 [3072], replicated, may hold values from -1.25 to 1.25
- teacher_contract_weight: bfloat16 [3072, 768], replicated, may hold values from -0.109375 to 0.109375
- teacher_contract_bias: float32 [768], replicated, may hold values from -1.25 to 1.25
- final_gain: float32 [768], replicated, may hold values from 0.5 to 1.5
- final_shift: float32 [768], replicated, may hold values from -1.25 to 1.25
- embedding: bfloat16 [32768, 768], P('blk'), may hold values from -0.8984375 to 0.8984375
Outputs:
- kl_rows: float32 [8192], P(('dp', 'blk'))
- input_grad: float32 [8192, 768], P(('dp', 'blk'))
- grad_first_gain: float32 [768], P('dp')
- grad_first_shift: float32 [768], P('dp')
- grad_project_in: float32 [768, 2304], P('dp')
- grad_query_value_bias: float32 [1536], P('dp')
- grad_attend_out: float32 [768, 768], P('dp')
- grad_attend_bias: float32 [768], P('dp')
- grad_second_gain: float32 [768], P('dp')
- grad_second_shift: float32 [768], P('dp')
- grad_expand_weight: float32 [768, 3072], P('dp')
- grad_expand_bias: float32 [3072], P('dp')
- grad_contract_weight: float32 [3072, 768], P('dp')
- grad_contract_bias: float32 [768], P('dp')
Inputs may be any that keep to these rules, and one draw needn't show every extreme that they name: `doc_lengths`: each stream's lengths sum to 512; one document of each stream has exactly 384 positions.
All inputs are finite; a program needn't handle non-finite values.
Results may differ from a plain program's by a relative error of at most 0.015.
Values may be sent and summed in bfloat16 or wider, within the bound.
No kernel may reach another device: no remote copies, remote signals or barrier semaphores. Data moves between devices by JAX's collectives and lax.ppermute only.
A program may use at most 320 MiB of HBM per device.

v0:
```python
import functools

import jax
import jax.numpy as jnp
from jax import lax
from jax.experimental import pallas as pl
from jax.experimental.pallas import tpu as pltpu
from jax.sharding import PartitionSpec as P

HEADS = 12
HEAD_DIM = 64
TABLE_SPAN = 2048
MASKS = (1, 2, 4, 8)
MASKS_B = (1, 4, 2, 8)


negative = -1e30


def layer_norm(value, gain, shift):
    centre = value - jnp.mean(value, axis=-1, keepdims=True)
    return (
        centre * lax.rsqrt(jnp.mean(centre * centre, axis=-1, keepdims=True) + 1e-05) * gain + shift
    )


def doc_numbers(lengths, count):
    ends = jnp.cumsum(lengths)
    places = jnp.arange(count, dtype=jnp.int32)
    return jnp.sum((places[:, None] >= ends[None, :]).astype(jnp.int32), axis=1)


def dense(left, right):
    return jnp.dot(left, right, preferred_element_type=jnp.float32)


def split_heads(value):
    return value.reshape(value.shape[0], HEADS, HEAD_DIM)


def input_side(inputs, gain, shift, project_in, qv_bias):
    width = inputs.shape[1]
    normed = layer_norm(inputs, gain, shift).astype(jnp.bfloat16)
    bias = jnp.concatenate([qv_bias[:width], jnp.zeros((width,), jnp.float32), qv_bias[width:]])
    joined = (dense(normed, project_in) + bias).astype(jnp.bfloat16)
    return (normed, joined[:, :width], joined[:, width : 2 * width], joined[:, 2 * width :])


def output_side(
    inputs,
    mixed_low,
    attend_out,
    attend_bias,
    second_gain,
    second_shift,
    expand_weight,
    expand_bias,
    contract_weight,
    contract_bias,
):
    after = inputs + dense(mixed_low, attend_out) + attend_bias
    normed = layer_norm(after, second_gain, second_shift).astype(jnp.bfloat16)
    inner = dense(normed, expand_weight) + expand_bias
    active = jax.nn.gelu(inner, approximate=True).astype(jnp.bfloat16)
    final = after + dense(active, contract_weight) + contract_bias
    return (after, normed, inner, active, final)


def online(state, query, keys, values, allowed):
    top, mass, summed = state
    scores = (
        jnp.einsum(
            "qhd,khd->hqk",
            split_heads(query),
            split_heads(keys),
            preferred_element_type=jnp.float32,
        )
        * 0.125
    )
    scores = jnp.where(allowed[None], scores, negative)
    new_top = jnp.maximum(top, jnp.max(scores, axis=-1))
    factor = jnp.exp(top - new_top)
    weights = jnp.where(allowed[None], jnp.exp(scores - new_top[..., None]), 0.0)
    mass = mass * factor + jnp.sum(weights, axis=-1)
    summed = summed * factor[..., None] + jnp.einsum(
        "hqk,khd->hqd",
        weights.astype(jnp.bfloat16),
        split_heads(values),
        preferred_element_type=jnp.float32,
    )
    return (new_top, mass, summed)


def score_grads(query_heads, grad_heads, log_norm, balance, key_block, value_block, allowed):
    scores = (
        jnp.einsum("qhd,khd->hqk", query_heads, key_block, preferred_element_type=jnp.float32)
        * 0.125
    )
    probs = jnp.where(allowed[None], jnp.exp(scores - log_norm[..., None]), 0.0)
    grad_probs = jnp.einsum(
        "qhd,khd->hqk", grad_heads, value_block, preferred_element_type=jnp.float32
    )
    grad_scores = (probs * (grad_probs - balance[..., None])).astype(jnp.bfloat16)
    return (probs, grad_scores)


def partial_stats(rows_teacher, rows_student, table):
    half_t = jnp.einsum("rd,vd->rv", rows_teacher, table, preferred_element_type=jnp.float32) * 0.5
    half_s = jnp.einsum("rd,vd->rv", rows_student, table, preferred_element_type=jnp.float32) * 0.5
    top_t = jnp.max(half_t, axis=-1)
    expo_t = jnp.exp(half_t - top_t[:, None])
    top_s = jnp.max(half_s, axis=-1)
    return (
        top_t,
        jnp.sum(expo_t, axis=-1),
        jnp.sum(expo_t * (half_t - half_s), axis=-1),
        top_s,
        jnp.sum(jnp.exp(half_s - top_s[:, None]), axis=-1),
    )


def combine(first_stats, second_stats):
    top_t = jnp.maximum(first_stats[0], second_stats[0])
    right_weight = jnp.exp(second_stats[0] - top_t)
    top_s = jnp.maximum(first_stats[3], second_stats[3])
    return (
        top_t,
        second_stats[1] * right_weight,
        second_stats[2] * right_weight,
        top_s,
        second_stats[4] * jnp.exp(second_stats[3] - top_s),
    )


def row_gradient(rows_teacher, rows_student, table, norm_t, norm_s):
    half_t = jnp.einsum("rd,vd->rv", rows_teacher, table, preferred_element_type=jnp.float32) * 0.5
    half_s = jnp.einsum("rd,vd->rv", rows_student, table, preferred_element_type=jnp.float32) * 0.5
    change = ((jnp.exp(half_s - norm_s[:, None]) - jnp.exp(half_t - norm_t[:, None])) * 0.5).astype(
        jnp.bfloat16
    )
    return dense(change, table)


def local_general(
    hidden,
    doc_lengths,
    student_first_gain,
    student_first_shift,
    student_project_in,
    student_query_value_bias,
    student_attend_out,
    student_attend_bias,
    student_second_gain,
    student_second_shift,
    student_expand_weight,
    student_expand_bias,
    student_contract_weight,
    student_contract_bias,
    teacher_first_gain,
    teacher_first_shift,
    teacher_project_in,
    teacher_query_value_bias,
    teacher_attend_out,
    teacher_attend_bias,
    teacher_second_gain,
    teacher_second_shift,
    teacher_expand_weight,
    teacher_expand_bias,
    teacher_contract_weight,
    teacher_contract_bias,
    final_gain,
    final_shift,
    embedding,
):
    rows, width = hidden.shape
    blocks = lax.axis_size("blk")
    stream = rows * blocks
    first = lax.axis_index("blk") * rows
    last_place = first + rows - 1
    docs = doc_numbers(doc_lengths[0], stream)
    own_places = first + jnp.arange(rows, dtype=jnp.int32)
    own_docs = lax.dynamic_slice_in_dim(docs, first, rows)
    inputs = hidden.astype(jnp.float32)
    normed_s, query_s, keys_s, values_s = input_side(
        inputs,
        student_first_gain,
        student_first_shift,
        student_project_in,
        student_query_value_bias,
    )
    normed_t, query_t, keys_t, values_t = input_side(
        inputs,
        teacher_first_gain,
        teacher_first_shift,
        teacher_project_in,
        teacher_query_value_bias,
    )

    def allowed_for(begin):
        key_places = begin + jnp.arange(rows, dtype=jnp.int32)
        key_docs = lax.dynamic_slice_in_dim(docs, begin, rows)
        return (key_places[None, :] <= own_places[:, None]) & (
            key_docs[None, :] == own_docs[:, None]
        )

    start_state = (
        jnp.full((HEADS, rows), negative, jnp.float32),
        jnp.zeros((HEADS, rows), jnp.float32),
        jnp.zeros((HEADS, rows, HEAD_DIM), jnp.float32),
    )
    carry = (start_state, start_state)
    pieces = (
        lax.all_gather(keys_s, "blk", axis=0, tiled=True),
        lax.all_gather(values_s, "blk", axis=0, tiled=True),
        lax.all_gather(keys_t, "blk", axis=0, tiled=True),
        lax.all_gather(values_t, "blk", axis=0, tiled=True),
    )
    count = pieces[0].shape[0]
    stacked = tuple((member.reshape(count // rows, rows, width) for member in pieces))
    begins = rows * jnp.arange(count // rows, dtype=jnp.int32)

    def step(state, item):
        piece_keys_s, piece_values_s, piece_keys_t, piece_values_t, begin = item

        def step_compute(inner_state):
            allowed = allowed_for(begin)
            return (
                online(inner_state[0], query_s, piece_keys_s, piece_values_s, allowed),
                online(inner_state[1], query_t, piece_keys_t, piece_values_t, allowed),
            )

        return (
            lax.cond(begin <= last_place, step_compute, lambda inner_state: inner_state, state),
            None,
        )

    carry, _ = lax.scan(step, carry, stacked + (begins,))
    state_s, state_t = carry
    out_heads_s = state_s[2] / state_s[1][..., None]
    attn_norm = state_s[0] + jnp.log(state_s[1])
    mixed_low_s = out_heads_s.transpose(1, 0, 2).reshape(rows, width).astype(jnp.bfloat16)
    mixed_low_t = (
        (state_t[2] / state_t[1][..., None])
        .transpose(1, 0, 2)
        .reshape(rows, width)
        .astype(jnp.bfloat16)
    )
    after_s, normed_two_s, inner_s, active_s, final_s = output_side(
        inputs,
        mixed_low_s,
        student_attend_out,
        student_attend_bias,
        student_second_gain,
        student_second_shift,
        student_expand_weight,
        student_expand_bias,
        student_contract_weight,
        student_contract_bias,
    )
    after_t, normed_two_t, inner_t, active_t, final_t = output_side(
        inputs,
        mixed_low_t,
        teacher_attend_out,
        teacher_attend_bias,
        teacher_second_gain,
        teacher_second_shift,
        teacher_expand_weight,
        teacher_expand_bias,
        teacher_contract_weight,
        teacher_contract_bias,
    )
    rows_s = layer_norm(final_s, final_gain, final_shift).astype(jnp.bfloat16)
    rows_t = layer_norm(final_t, final_gain, final_shift).astype(jnp.bfloat16)
    identity = (
        jnp.full((rows,), negative, jnp.float32),
        jnp.zeros((rows,), jnp.float32),
        jnp.zeros((rows,), jnp.float32),
        jnp.full((rows,), negative, jnp.float32),
        jnp.zeros((rows,), jnp.float32),
    )
    merged = combine(
        identity,
        partial_stats(rows_t, rows_s, lax.all_gather(embedding, "blk", axis=0, tiled=True)),
    )
    norm_t = merged[0] + jnp.log(merged[1])
    norm_s = merged[3] + jnp.log(merged[4])
    kl_rows = merged[2] / merged[1] - norm_t + norm_s
    grad_final = row_gradient(
        rows_t, rows_s, lax.all_gather(embedding, "blk", axis=0, tiled=True), norm_t, norm_s
    )
    _, final_back = jax.vjp(layer_norm, final_s, final_gain, final_shift)
    grad_y = final_back(grad_final)[0]
    grad_m = grad_y.astype(jnp.bfloat16)
    grad_contract_weight = jnp.einsum(
        "rf,rd->fd", active_s, grad_m, preferred_element_type=jnp.float32
    )
    grad_contract_bias = jnp.sum(grad_m.astype(jnp.float32), axis=0)
    grad_active = jnp.einsum(
        "rd,fd->rf", grad_m, student_contract_weight, preferred_element_type=jnp.float32
    )
    _, gelu_back = jax.vjp(lambda value: jax.nn.gelu(value, approximate=True), inner_s)
    grad_inner = gelu_back(grad_active)[0].astype(jnp.bfloat16)
    grad_expand_weight = jnp.einsum(
        "rd,rf->df", normed_two_s, grad_inner, preferred_element_type=jnp.float32
    )
    grad_expand_bias = jnp.sum(grad_inner.astype(jnp.float32), axis=0)
    grad_normed_two = jnp.einsum(
        "rf,df->rd", grad_inner, student_expand_weight, preferred_element_type=jnp.float32
    )
    _, second_back = jax.vjp(layer_norm, after_s, student_second_gain, student_second_shift)
    grad_after_norm, grad_second_gain, grad_second_shift = second_back(grad_normed_two)
    grad_after = grad_y + grad_after_norm
    grad_branch = grad_after.astype(jnp.bfloat16)
    grad_attend_out = jnp.einsum(
        "rc,rd->cd", mixed_low_s, grad_branch, preferred_element_type=jnp.float32
    )
    grad_attend_bias = jnp.sum(grad_branch.astype(jnp.float32), axis=0)
    grad_mixed = jnp.einsum(
        "rd,cd->rc", grad_branch, student_attend_out, preferred_element_type=jnp.float32
    ).astype(jnp.bfloat16)
    keys_all, values_all = (
        lax.all_gather(keys_s, "blk", axis=0, tiled=True),
        lax.all_gather(values_s, "blk", axis=0, tiled=True),
    )
    grad_heads = split_heads(grad_mixed)
    query_heads = split_heads(query_s)
    balance = jnp.sum(grad_heads.astype(jnp.float32).transpose(1, 0, 2) * out_heads_s, axis=-1)
    begins = rows * jnp.arange(blocks, dtype=jnp.int32)
    zero_query = jnp.zeros((rows, HEADS, HEAD_DIM), jnp.float32)

    def back_step(grad_query, begin):
        key_block = split_heads(lax.dynamic_slice_in_dim(keys_all, begin, rows, 0))
        value_block = split_heads(lax.dynamic_slice_in_dim(values_all, begin, rows, 0))

        def back_compute(total):
            probs, grad_scores = score_grads(
                query_heads,
                grad_heads,
                attn_norm,
                balance,
                key_block,
                value_block,
                allowed_for(begin),
            )
            total = (
                total
                + jnp.einsum(
                    "hqk,khd->qhd", grad_scores, key_block, preferred_element_type=jnp.float32
                )
                * 0.125
            )
            grad_keys = (
                jnp.einsum(
                    "hqk,qhd->khd", grad_scores, query_heads, preferred_element_type=jnp.float32
                )
                * 0.125
            )
            grad_values = jnp.einsum(
                "hqk,qhd->khd",
                probs.astype(jnp.bfloat16),
                grad_heads,
                preferred_element_type=jnp.float32,
            )
            return (
                total,
                jnp.concatenate(
                    [grad_keys.reshape(rows, width), grad_values.reshape(rows, width)], axis=1
                ),
            )

        def skip(total):
            return (total, jnp.zeros((rows, 2 * width), jnp.float32))

        return lax.cond(begin <= last_place, back_compute, skip, grad_query)

    grad_query, key_terms = lax.scan(back_step, zero_query, begins)
    key_value_grad = lax.psum_scatter(
        key_terms.reshape(stream, 2 * width).astype(jnp.bfloat16),
        "blk",
        scatter_dimension=0,
        tiled=True,
    ).astype(jnp.float32)
    grad_keys_low = key_value_grad[:, :width].astype(jnp.bfloat16)
    grad_values_low = key_value_grad[:, width:].astype(jnp.bfloat16)
    grad_query_low = grad_query.reshape(rows, width).astype(jnp.bfloat16)
    grad_joined = jnp.concatenate([grad_query_low, grad_keys_low, grad_values_low], axis=1)
    grad_project_in = jnp.einsum(
        "rd,rc->dc", normed_s, grad_joined, preferred_element_type=jnp.float32
    )
    grad_query_value_bias = jnp.concatenate(
        [
            jnp.sum(grad_query_low.astype(jnp.float32), axis=0),
            jnp.sum(grad_values_low.astype(jnp.float32), axis=0),
        ]
    )
    grad_normed = jnp.einsum(
        "rc,dc->rd", grad_joined, student_project_in, preferred_element_type=jnp.float32
    )
    _, first_back = jax.vjp(layer_norm, inputs, student_first_gain, student_first_shift)
    grad_inputs_norm, grad_first_gain, grad_first_shift = first_back(grad_normed)
    input_grad = grad_after + grad_inputs_norm
    shares = (
        lax.psum_scatter(
            grad_first_gain.astype(jnp.bfloat16), "dp", scatter_dimension=0, tiled=True
        ).astype(jnp.float32),
        lax.psum_scatter(
            grad_first_shift.astype(jnp.bfloat16), "dp", scatter_dimension=0, tiled=True
        ).astype(jnp.float32),
        lax.psum_scatter(
            grad_project_in.astype(jnp.bfloat16), "dp", scatter_dimension=0, tiled=True
        ).astype(jnp.float32),
        lax.psum_scatter(
            grad_query_value_bias.astype(jnp.bfloat16), "dp", scatter_dimension=0, tiled=True
        ).astype(jnp.float32),
        lax.psum_scatter(
            grad_attend_out.astype(jnp.bfloat16), "dp", scatter_dimension=0, tiled=True
        ).astype(jnp.float32),
        lax.psum_scatter(
            grad_attend_bias.astype(jnp.bfloat16), "dp", scatter_dimension=0, tiled=True
        ).astype(jnp.float32),
        lax.psum_scatter(
            grad_second_gain.astype(jnp.bfloat16), "dp", scatter_dimension=0, tiled=True
        ).astype(jnp.float32),
        lax.psum_scatter(
            grad_second_shift.astype(jnp.bfloat16), "dp", scatter_dimension=0, tiled=True
        ).astype(jnp.float32),
        lax.psum_scatter(
            grad_expand_weight.astype(jnp.bfloat16), "dp", scatter_dimension=0, tiled=True
        ).astype(jnp.float32),
        lax.psum_scatter(
            grad_expand_bias.astype(jnp.bfloat16), "dp", scatter_dimension=0, tiled=True
        ).astype(jnp.float32),
        lax.psum_scatter(
            grad_contract_weight.astype(jnp.bfloat16), "dp", scatter_dimension=0, tiled=True
        ).astype(jnp.float32),
        lax.psum_scatter(
            grad_contract_bias.astype(jnp.bfloat16), "dp", scatter_dimension=0, tiled=True
        ).astype(jnp.float32),
    )
    summed = (
        lax.psum(shares[0].astype(jnp.bfloat16), "blk").astype(jnp.float32),
        lax.psum(shares[1].astype(jnp.bfloat16), "blk").astype(jnp.float32),
        lax.psum(shares[2].astype(jnp.bfloat16), "blk").astype(jnp.float32),
        lax.psum(shares[3].astype(jnp.bfloat16), "blk").astype(jnp.float32),
        lax.psum(shares[4].astype(jnp.bfloat16), "blk").astype(jnp.float32),
        lax.psum(shares[5].astype(jnp.bfloat16), "blk").astype(jnp.float32),
        lax.psum(shares[6].astype(jnp.bfloat16), "blk").astype(jnp.float32),
        lax.psum(shares[7].astype(jnp.bfloat16), "blk").astype(jnp.float32),
        lax.psum(shares[8].astype(jnp.bfloat16), "blk").astype(jnp.float32),
        lax.psum(shares[9].astype(jnp.bfloat16), "blk").astype(jnp.float32),
        lax.psum(shares[10].astype(jnp.bfloat16), "blk").astype(jnp.float32),
        lax.psum(shares[11].astype(jnp.bfloat16), "blk").astype(jnp.float32),
    )
    return (
        kl_rows,
        input_grad,
        summed[0],
        summed[1],
        summed[2],
        summed[3],
        summed[4],
        summed[5],
        summed[6],
        summed[7],
        summed[8],
        summed[9],
        summed[10],
        summed[11],
    )


def nt(left, right):
    return lax.dot_general(
        left, right, (((1,), (1,)), ((), ())), preferred_element_type=jnp.float32
    )


def tn(left, right):
    return lax.dot_general(
        left, right, (((0,), (0,)), ((), ())), preferred_element_type=jnp.float32
    )


def normalise(value):
    centre = value - jnp.mean(value, axis=-1, keepdims=True)
    scale = lax.rsqrt(jnp.mean(centre * centre, axis=-1, keepdims=True) + 1e-05)
    return (centre * scale, scale)


def norm_back(normed, scale, gain, grad):
    weighted = grad * gain
    return scale * (
        weighted
        - jnp.mean(weighted, axis=-1, keepdims=True)
        - normed * jnp.mean(weighted * normed, axis=-1, keepdims=True)
    )


def starts_of(lengths_ref, count):
    places = lax.broadcasted_iota(jnp.int32, (1, count), 1)
    start = jnp.zeros((1, count), jnp.int32)
    end = jnp.int32(0)
    for index in range(lengths_ref.shape[1]):
        end = end + lengths_ref[0, index]
        start = jnp.where(places >= end, jnp.maximum(start, end), start)
    return start


def in_stream_order(target, own_ref, other_ref, blk):
    rows = own_ref.shape[0]
    target[pl.ds(pl.multiple_of(blk * rows, rows), rows), :] = own_ref[...].astype(target.dtype)
    target[pl.ds(pl.multiple_of((1 - blk) * rows, rows), rows), :] = other_ref[...].astype(
        target.dtype
    )


def head_mask(shape, which):
    lanes = lax.broadcasted_iota(jnp.int32, shape, 1)
    return (lanes >= HEAD_DIM) if which else (lanes < HEAD_DIM)


def forward_kernel(train, *refs):
    (
        place_ref,
        lengths_ref,
        own_ref,
        other_ref,
    ) = refs[:4]
    (
        first_gain,
        first_shift,
        qv_bias,
        attend_bias,
        second_gain,
        second_shift,
        expand_bias,
        contract_bias,
        final_gain,
        final_shift,
    ) = (as_row(ref) for ref in refs[4:14])
    weights_hbm = refs[14:18]
    rest = refs[18:]
    if train:
        rows_out, kept_hbm, rest = rest[0], rest[1:10], rest[10:]
    else:
        rows_out, kept_hbm, rest = rest[0], (), rest[1:]
    wpi, wao, we, wc = rest[:4]
    normed_v, joined_v, probs_v, mixed_v, after_v, normed_two_v, slope_v, active_v, y_v = rest[4:13]
    x_v, bias_v, weight_sem, out_sem, probs_sem = rest[13:]
    kept = (normed_v, joined_v, probs_v, mixed_v, after_v, normed_two_v, slope_v, active_v, y_v)
    loads = [
        pltpu.make_async_copy(source, target, weight_sem.at[index])
        for index, (source, target) in enumerate(zip(weights_hbm, (wpi, wao, we, wc)))
    ]
    stores = []

    def save(index, *at):
        if train:
            source, target = kept[index], kept_hbm[index]
            if at:
                source, target = source.at[at], target.at[at]
            store = pltpu.make_async_copy(source, target, out_sem.at[len(stores)])
            store.start()
            stores.append(store)

    for load in loads:
        load.start()
    blk = place_ref[1]
    in_stream_order(x_v, own_ref, other_ref, blk)
    count, width = x_v.shape
    block = own_ref.shape[0]
    normed, _ = normalise(x_v[...])
    normed_v[...] = (normed * first_gain + first_shift).astype(jnp.bfloat16)
    save(0)
    start = starts_of(lengths_ref, count)
    keys_at = lax.broadcasted_iota(jnp.int32, (count, count), 0)
    queries_at = lax.broadcasted_iota(jnp.int32, (count, count), 1)
    bias_v[...] = jnp.where((keys_at <= queries_at) & (keys_at >= start), 0.0, negative)
    loads[0].wait()
    for part in range(3):
        span = slice(part * width, (part + 1) * width)
        value = dense(normed_v[...], wpi[:, span])
        if part == 0:
            value = value + qv_bias[:, :width]
        if part == 2:
            value = value + qv_bias[:, width:]
        joined_v[:, span] = value.astype(jnp.bfloat16)
    save(1)
    pair = 2 * HEAD_DIM
    pairs = width // pair

    def attend(index, _):
        column = pl.ds(pl.multiple_of(index * pair, pair), pair)
        query = joined_v[:, column] * jnp.bfloat16(0.125)
        keys = joined_v[:, pl.ds(pl.multiple_of(width + index * pair, pair), pair)]
        values = joined_v[:, pl.ds(pl.multiple_of(2 * width + index * pair, pair), pair)]
        for piece in range(count // block):
            span = slice(piece * block, (piece + 1) * block)
            reach = (piece + 1) * block
            both = []
            for which in range(2):
                mine = jnp.where(
                    head_mask((block, pair), which), query[span], jnp.bfloat16(0.0)
                )
                scores = nt(keys[:reach], mine) + bias_v[:reach, span]
                expo = jnp.exp(scores - jnp.max(scores, axis=0, keepdims=True))
                probs = expo * (1.0 / jnp.sum(expo, axis=0, keepdims=True))
                probs = probs.astype(jnp.bfloat16)
                if train:
                    probs_v[2 * index + which, :reach, span] = probs
                both.append(tn(probs, values[:reach]))
            mixed_v[span, column] = jnp.where(
                head_mask((block, pair), 0), both[0], both[1]
            ).astype(jnp.bfloat16)
        if train:
            heads = pl.ds(2 * index, 2)
            pltpu.make_async_copy(
                probs_v.at[heads], kept_hbm[2].at[heads], probs_sem.at[index]
            ).start()
        return 0

    lax.fori_loop(0, pairs, attend, 0, unroll=3)
    if train:
        for index in range(pairs):
            heads = pl.ds(2 * index, 2)
            stores.append(
                pltpu.make_async_copy(
                    probs_v.at[heads], kept_hbm[2].at[heads], probs_sem.at[index]
                )
            )
    save(3)
    loads[1].wait()
    after_v[...] = x_v[...] + dense(mixed_v[...], wao[...]) + attend_bias
    save(4)
    normed, _ = normalise(after_v[...])
    normed_two_v[...] = (normed * second_gain + second_shift).astype(jnp.bfloat16)
    save(5)
    loads[2].wait()
    loads[3].wait()
    hidden_width = we.shape[1]
    total = after_v[...] + contract_bias
    root = 0.7978845608028654
    for part in range(hidden_width // width):
        span = slice(part * width, (part + 1) * width)
        inner = dense(normed_two_v[...], we[:, span]) + expand_bias[:, span]
        square = inner * inner
        bent = jnp.tanh(root * (inner + 0.044715 * (square * inner)))
        upper = 0.5 * (1.0 + bent)
        active = (inner * upper).astype(jnp.bfloat16)
        if train:
            active_v[:, span] = active
            slope_v[:, span] = (
                upper
                + (0.5 * root) * inner * (1.0 - bent * bent) * (1.0 + (3 * 0.044715) * square)
            ).astype(jnp.bfloat16)
            save(6, slice(None), pl.ds(part * width, width))
            save(7, slice(None), pl.ds(part * width, width))
        total = total + dense(active, wc[span, :])
    if train:
        y_v[...] = total
    save(8)
    normed, _ = normalise(total)
    rows_out[...] = (normed * final_gain + final_shift).astype(jnp.bfloat16) * jnp.bfloat16(0.5)
    if train:
        for store in stores:
            store.wait()


def carrying(kernel, inputs, outputs, carried):
    def body(*refs):
        rest = refs[inputs + carried :]
        kernel(*refs[:inputs], *rest[:outputs], *rest[outputs + carried :])

    return body


def shapes_of(carry):
    return [jax.ShapeDtypeStruct(item.shape, item.dtype) for item in carry]


def aliases(inputs, outputs, carry):
    return {inputs + index: outputs + index for index in range(len(carry))}


def as_row(ref):
    return ref[...].reshape(1, ref.shape[0])


def whole_vmem():
    return pl.BlockSpec(memory_space=pltpu.VMEM)


def in_place():
    return pl.BlockSpec(memory_space=pl.ANY)


def far(*arrays):
    return [pltpu.with_memory_space_constraint(array, pltpu.HBM) for array in arrays]


def scalars():
    return pl.BlockSpec(memory_space=pltpu.SMEM)


def forward(train, place, lengths, own, other, vectors, weights):
    rows, width = own.shape
    count = 2 * rows
    hidden_width = weights[2].shape[1]
    low, full = jnp.bfloat16, jnp.float32
    kept = [
        ((count, width), low),
        ((count, 3 * width), low),
        ((HEADS, count, count), low),
        ((count, width), low),
        ((count, width), full),
        ((count, width), low),
        ((count, hidden_width), low),
        ((count, hidden_width), low),
        ((count, width), full),
    ]
    small = ((8, 128), low)
    scratch = [kept[0], kept[1], kept[2] if train else ((1, 8, 128), low), kept[3], kept[4], kept[5]]
    scratch += [kept[6], kept[7], kept[8]] if train else [small, small, ((8, 128), full)]
    out_shape = [jax.ShapeDtypeStruct((count, width), low)]
    out_specs = [whole_vmem()]
    if train:
        out_shape += [jax.ShapeDtypeStruct(*item) for item in kept]
        out_specs += [in_place()] * len(kept)
    return pl.pallas_call(
        functools.partial(forward_kernel, train),
        in_specs=[scalars(), scalars()] + [whole_vmem()] * 12 + [in_place()] * 4,
        out_specs=out_specs,
        out_shape=out_shape,
        scratch_shapes=[pltpu.VMEM(item.shape, low) for item in weights]
        + [pltpu.VMEM(*item) for item in scratch]
        + [
            pltpu.VMEM((count, width), full),
            pltpu.VMEM((count, count), full),
            pltpu.SemaphoreType.DMA((4,)),
            pltpu.SemaphoreType.DMA((32,)),
            pltpu.SemaphoreType.DMA((HEADS // 2,)),
        ],
        compiler_params=pltpu.CompilerParams(vmem_limit_bytes=(54 if train else 44) << 20),
        cost_estimate=pl.CostEstimate(
            flops=8_000_000_000, bytes_accessed=20_000_000, transcendentals=0
        ),
        name="forward_student" if train else "forward_teacher",
    )(place, lengths, own, other, *far(*vectors, *weights))


def logits_kernel(student_ref, teacher_ref, table_ref, diff_ref, expo_ref, stats_ref, sums_ref):
    count = student_ref.shape[0]
    span = table_ref.shape[0] // 8
    lanes = lax.broadcasted_iota(jnp.int32, (count, 128), 1)
    packed = jnp.zeros((count, 128), jnp.float32)
    for part in range(8):
        where = slice(part * span, (part + 1) * span)
        table = table_ref[where, :]
        half_s = nt(student_ref[...], table)
        top_s = jnp.max(half_s, axis=1, keepdims=True)
        expo_s = jnp.exp(half_s - top_s)
        mass_s = jnp.sum(expo_s, axis=1, keepdims=True)
        half_t = nt(teacher_ref[...], table)
        top_t = jnp.max(half_t, axis=1, keepdims=True)
        expo_t = jnp.exp(half_t - top_t)
        mass_t = jnp.sum(expo_t, axis=1, keepdims=True)
        cross = jnp.sum(expo_t * (half_t - half_s), axis=1, keepdims=True)
        diff_ref[:, where] = (expo_s * (mass_t / mass_s) - expo_t).astype(jnp.bfloat16)
        expo_ref[:, where] = expo_t.astype(jnp.bfloat16)
        for index, column in enumerate((top_s, mass_s, top_t, mass_t, cross)):
            packed = jnp.where(lanes == 8 * index + part, column, packed)
    stats = packed.T
    stats_ref[0] = stats[:40]
    top_s, mass_s, top_t, mass_t, cross = (stats[8 * i : 8 * i + 8] for i in range(5))

    @pl.when(pl.program_id(0) == 0)
    def _():
        row = lax.broadcasted_iota(jnp.int32, sums_ref.shape, 0)
        sums_ref[...] = jnp.where((row == 0) | (row == 2), negative, 0.0)

    old = sums_ref[...]
    new_s = jnp.maximum(old[0:1], jnp.max(top_s, axis=0, keepdims=True))
    new_t = jnp.maximum(old[2:3], jnp.max(top_t, axis=0, keepdims=True))
    keep_s = jnp.exp(old[0:1] - new_s)
    keep_t = jnp.exp(old[2:3] - new_t)
    scale_s = jnp.exp(top_s - new_s)
    scale_t = jnp.exp(top_t - new_t)
    sums_ref[0:1] = new_s
    sums_ref[1:2] = old[1:2] * keep_s + jnp.sum(mass_s * scale_s, axis=0, keepdims=True)
    sums_ref[2:3] = new_t
    sums_ref[3:4] = old[3:4] * keep_t + jnp.sum(mass_t * scale_t, axis=0, keepdims=True)
    sums_ref[4:5] = old[4:5] * keep_t + jnp.sum(cross * scale_t, axis=0, keepdims=True)


def logits_phase(student, teacher, table):
    count, width = student.shape
    entries = table.shape[0]
    span = TABLE_SPAN
    steps = entries // span
    rows = pl.BlockSpec((count, width), lambda j: (0, 0))
    wide = pl.BlockSpec((count, span), lambda j: (0, j))
    return pl.pallas_call(
        logits_kernel,
        grid=(steps,),
        in_specs=[rows, rows, pl.BlockSpec((span, width), lambda j: (j, 0))],
        out_specs=[
            wide,
            wide,
            pl.BlockSpec((1, 40, count), lambda j: (j, 0, 0)),
            pl.BlockSpec((8, count), lambda j: (0, 0)),
        ],
        out_shape=[
            jax.ShapeDtypeStruct((count, entries), jnp.bfloat16),
            jax.ShapeDtypeStruct((count, entries), jnp.bfloat16),
            jax.ShapeDtypeStruct((steps, 40, count), jnp.float32),
            jax.ShapeDtypeStruct((8, count), jnp.float32),
        ],
        compiler_params=pltpu.CompilerParams(vmem_limit_bytes=24 << 20),
        cost_estimate=pl.CostEstimate(
            flops=4 * count * width * entries, bytes_accessed=60_000_000, transcendentals=0
        ),
        name="logits_phase",
    )(student, teacher, *far(table))


def joined_norms(own, other):
    top_s = jnp.maximum(own[0:1], other[0:1])
    top_t = jnp.maximum(own[2:3], other[2:3])
    own_t, other_t = jnp.exp(own[2:3] - top_t), jnp.exp(other[2:3] - top_t)
    mass_s = own[1:2] * jnp.exp(own[0:1] - top_s) + other[1:2] * jnp.exp(other[0:1] - top_s)
    mass_t = own[3:4] * own_t + other[3:4] * other_t
    cross = own[4:5] * own_t + other[4:5] * other_t
    norm_s = top_s + jnp.log(mass_s)
    norm_t = top_t + jnp.log(mass_t)
    return (norm_s, norm_t, cross / mass_t - norm_t + norm_s)


def gradient_kernel(
    half,
    diff_ref,
    expo_ref,
    table_ref,
    stats_ref,
    own_ref,
    other_ref,
    total_ref,
    low_ref,
    kl_ref,
    norms,
):
    step = pl.program_id(0)
    count = diff_ref.shape[0]
    mine = slice(half * count, (half + 1) * count)

    @pl.when(step == 0)
    def _():
        norm_s, norm_t, divergence = joined_norms(own_ref[:, mine], other_ref[:, mine])
        norms[0:1] = norm_s
        norms[1:2] = norm_t
        kl_ref[...] = divergence
        total_ref[...] = jnp.zeros_like(total_ref)

    top_s, mass_s, top_t, mass_t = (stats_ref[0, 8 * i : 8 * i + 8, mine] for i in range(4))
    first = 0.5 * jnp.exp(top_s - norms[0:1]) * mass_s / mass_t
    second = first - 0.5 * jnp.exp(top_t - norms[1:2])
    factors = jnp.concatenate([first, second, jnp.zeros((112, count), jnp.float32)], axis=0).T
    span = table_ref.shape[0] // 8
    total = total_ref[...]
    for group in range(2):
        pieces = []
        for part in range(4 * group, 4 * group + 4):
            where = slice(part * span, (part + 1) * span)
            pieces.append(
                (
                    diff_ref[:, where].astype(jnp.float32) * factors[:, part : part + 1]
                    + expo_ref[:, where].astype(jnp.float32) * factors[:, 8 + part : 9 + part]
                ).astype(jnp.bfloat16)
            )
        where = slice(4 * group * span, 4 * (group + 1) * span)
        total = total + dense(jnp.concatenate(pieces, axis=1), table_ref[where, :])
    total_ref[...] = total

    @pl.when(step == pl.num_programs(0) - 1)
    def _():
        low_ref[...] = total_ref[...].astype(jnp.bfloat16)


def gradient_phase(diff, expo, table, stats, own, other, half):
    count, entries = diff.shape
    rows = count // 2
    width = table.shape[1]
    span = TABLE_SPAN
    wide = pl.BlockSpec((rows, span), lambda j: (half, j))
    sums = pl.BlockSpec((8, count), lambda j: (0, 0))
    fixed = pl.BlockSpec((rows, width), lambda j: (0, 0))
    return pl.pallas_call(
        functools.partial(gradient_kernel, half),
        grid=(entries // span,),
        in_specs=[
            wide,
            wide,
            pl.BlockSpec((span, width), lambda j: (j, 0)),
            pl.BlockSpec((1, 40, count), lambda j: (j, 0, 0)),
            sums,
            sums,
        ],
        out_specs=[fixed, fixed, pl.BlockSpec((1, rows), lambda j: (0, 0))],
        out_shape=[
            jax.ShapeDtypeStruct((rows, width), jnp.float32),
            jax.ShapeDtypeStruct((rows, width), jnp.bfloat16),
            jax.ShapeDtypeStruct((1, rows), jnp.float32),
        ],
        scratch_shapes=[pltpu.VMEM((8, rows), jnp.float32)],
        compiler_params=pltpu.CompilerParams(vmem_limit_bytes=20 << 20),
        cost_estimate=pl.CostEstimate(
            flops=2 * count * width * entries, bytes_accessed=60_000_000, transcendentals=0
        ),
        name="gradient_second" if half else "gradient_first",
    )(diff, *far(expo, table), stats, own, other)


def position(device, masks):
    rest = masks[1:]
    place = jnp.int32(0) if not isinstance(device, int) else 0
    for index, mask in enumerate(rest):
        if isinstance(device, int):
            bit = (device // mask) % 2
        else:
            bit = lax.rem(lax.div(device, mask), 2)
        place = place + (bit << (len(rest) - 1 - index))
    return place


def place_shards(me, natural, keep, send, masks, first, shards, rows=slice(None)):
    mine = lax.rem(me, 2)
    place = position(me, masks)
    for pair in range(first // 2, (first + shards) // 2):
        target = lax.bitwise_xor(place, jnp.int32(position(2 * pair, masks)))
        keep[target, rows] = natural[2 * pair + mine, rows]
        send[target, rows] = natural[2 * pair + 1 - mine, rows]


def row_sums(value):
    return jnp.sum(value.astype(jnp.float32), axis=0, keepdims=True)


def back_to_norm(own_ref, other_ref, y_ref, gain):
    normed, scale = normalise(y_ref[...])
    grad = own_ref[...] + other_ref[...].astype(jnp.float32)
    return norm_back(normed, scale, as_row(gain), grad)


def feed_loads(wc_hbm, wc, slope_hbm, slope_v, rows, sems):
    hidden_width, width = wc.shape
    loads = []
    for part in range(hidden_width // width):
        span = pl.ds(part * width, width)
        loads.append(
            (
                pltpu.make_async_copy(wc_hbm.at[span], wc.at[span], sems.at[0, part]),
                pltpu.make_async_copy(
                    slope_hbm.at[rows, span], slope_v.at[:, span], sems.at[1, part]
                ),
            )
        )
    return loads


def feed_rows(dm, wc, slope_v, loads, dinner, rows, bias_out, bias_before):
    width = wc.shape[1]
    for part, pair in enumerate(loads):
        span = slice(part * width, (part + 1) * width)
        for load in pair:
            load.wait()
        value = nt(dm, wc[span, :]) * slope_v[:, span].astype(jnp.float32)
        value = value.astype(jnp.bfloat16)
        dinner[rows, span] = value
        before = 0.0 if bias_before is None else bias_before[:, span]
        bias_out[:, span] = before + row_sums(value)


def expand_loads(we_hbm, we, wao_hbm, wao, sems):
    width = we.shape[0]
    parts = we.shape[1] // width
    spans = [pl.ds(part * width, width) for part in range(parts)]
    return [
        pltpu.make_async_copy(we_hbm.at[:, span], we.at[:, span], sems.at[part])
        for part, span in enumerate(spans)
    ] + [pltpu.make_async_copy(wao_hbm, wao, sems.at[parts])]


def branch_rows(dinner, we, loads, after_ref, gain, dy):
    width = we.shape[0]
    dh2 = None
    for part, load in enumerate(loads[:-1]):
        span = slice(part * width, (part + 1) * width)
        load.wait()
        term = nt(dinner[:, span], we[:, span])
        dh2 = term if dh2 is None else dh2 + term
    normed, scale = normalise(after_ref[...])
    dafter = dy + norm_back(normed, scale, as_row(gain), dh2)
    return dafter, row_sums(dh2 * normed), row_sums(dh2)


def first_kernel(
    own_ref,
    other_ref,
    y_ref,
    after_ref,
    final_gain,
    second_gain,
    wc_hbm,
    we_hbm,
    wao_hbm,
    slope_hbm,
    dm_out,
    dinner_out,
    dafter_out,
    dbranch_out,
    dmixed_out,
    contract_bias_out,
    expand_bias_out,
    second_gain_out,
    second_shift_out,
    attend_bias_out,
    wc,
    we,
    wao,
    slope_v,
    feed_sem,
    branch_sem,
):
    count = own_ref.shape[0]
    feeding = feed_loads(wc_hbm, wc, slope_hbm, slope_v, pl.ds(0, count), feed_sem)
    branching = expand_loads(we_hbm, we, wao_hbm, wao, branch_sem)
    for pair in feeding:
        for load in pair:
            load.start()
    for load in branching:
        load.start()
    dy = back_to_norm(own_ref, other_ref, y_ref, final_gain)
    dm = dy.astype(jnp.bfloat16)
    dm_out[...] = dm
    contract_bias_out[...] = row_sums(dm)
    feed_rows(dm, wc, slope_v, feeding, dinner_out, slice(0, count), expand_bias_out, None)
    dafter, second_gain_out[...], second_shift_out[...] = branch_rows(
        dinner_out, we, branching, after_ref, second_gain, dy
    )
    dafter_out[...] = dafter
    dbranch = dafter.astype(jnp.bfloat16)
    dbranch_out[...] = dbranch
    attend_bias_out[...] = row_sums(dbranch)
    branching[-1].wait()
    dmixed_out[...] = nt(dbranch, wao[...]).astype(jnp.bfloat16)


def first_rows(own, other, y, after, final_gain, second_gain, wc, we, wao, slope):
    rows, width = own.shape
    hidden_width = wc.shape[0]
    low, full = jnp.bfloat16, jnp.float32
    parts = hidden_width // width

    def array(size, kind):
        return jax.ShapeDtypeStruct((rows, size), kind)

    def vector(size):
        return jax.ShapeDtypeStruct((1, size), full)

    top = pl.BlockSpec((rows, width), lambda i: (0, 0))
    return pl.pallas_call(
        first_kernel,
        grid=(1,),
        in_specs=[whole_vmem()] * 2 + [top] * 2 + [whole_vmem()] * 2 + [in_place()] * 4,
        out_specs=[whole_vmem()] * 10,
        out_shape=[
            array(width, low),
            array(hidden_width, low),
            array(width, full),
            array(width, low),
            array(width, low),
            vector(width),
            vector(hidden_width),
            vector(width),
            vector(width),
            vector(width),
        ],
        scratch_shapes=[
            pltpu.VMEM(wc.shape, low),
            pltpu.VMEM(we.shape, low),
            pltpu.VMEM(wao.shape, low),
            pltpu.VMEM((rows, hidden_width), low),
            pltpu.SemaphoreType.DMA((2, parts)),
            pltpu.SemaphoreType.DMA((parts + 1,)),
        ],
        compiler_params=pltpu.CompilerParams(vmem_limit_bytes=24 << 20),
        cost_estimate=pl.CostEstimate(
            flops=12_000_000_000, bytes_accessed=1_000_000, transcendentals=0
        ),
        name="first_rows",
    )(own, other, *far(y, after, final_gain, second_gain, wc, we, wao, slope))


def feed_kernel(
    place_ref,
    own_ref,
    other_ref,
    y_ref,
    final_gain,
    dm_first,
    normed_two_ref,
    contract_bias_first,
    expand_bias_first,
    wc_hbm,
    slope_hbm,
    active_hbm,
    dinner_hbm,
    cw_keep,
    cw_send,
    ew_keep,
    ew_send,
    dy_out,
    dinner_out,
    contract_bias_out,
    expand_bias_out,
    wc,
    slope_v,
    active_v,
    dinner_v,
    dm_v,
    cw_natural,
    ew_natural,
    feed_sem,
    load_sem,
    out_sem,
):
    me, blk = place_ref[0], place_ref[1]
    rows = own_ref.shape[0]
    second = slice(rows, 2 * rows)
    hidden_width, width = wc.shape
    parts = hidden_width // width
    part_width = width // 2
    shards = cw_natural.shape[0]
    chunk = width // shards
    feeding = feed_loads(wc_hbm, wc, slope_hbm, slope_v, pl.ds(rows, rows), feed_sem)
    early = pltpu.make_async_copy(dinner_hbm, dinner_v.at[pl.ds(0, rows)], load_sem.at[0])
    loads = [
        pltpu.make_async_copy(
            active_hbm.at[:, pl.ds(part * width, width)],
            active_v.at[:, pl.ds(part * width, width)],
            load_sem.at[1 + part],
        )
        for part in range(parts)
    ]
    for load in loads:
        load.start()
    for pair in feeding:
        for load in pair:
            load.start()
    early.start()
    dy = back_to_norm(own_ref, other_ref, y_ref, final_gain)
    dy_out[...] = dy
    dm = dy.astype(jnp.bfloat16)
    dm_v[:rows] = dm_first[...]
    dm_v[second] = dm
    contract_bias_out[...] = contract_bias_first[...] + row_sums(dm)
    dm_half = dm_v[:, pl.ds(pl.multiple_of(blk * part_width, part_width), part_width)]
    group = shards // parts
    for part in range(parts):
        span = slice(part * width, (part + 1) * width)
        loads[part].wait()
        value = tn(active_v[:, span], dm_half).astype(jnp.bfloat16)
        cw_natural[part * group : (part + 1) * group] = value.reshape(
            group, width // group, part_width
        )
        place_shards(me, cw_natural, cw_keep, cw_send, MASKS, part * group, group)
    feed_rows(dm, wc, slope_v, feeding, dinner_v, second, expand_bias_out, expand_bias_first)
    save = pltpu.make_async_copy(dinner_v.at[pl.ds(rows, rows)], dinner_out, out_sem.at[0])
    save.start()
    early.wait()
    for part in range(parts // 2):
        offset = pl.multiple_of(blk * (hidden_width // 2), width) + part * width
        value = tn(normed_two_ref[...], dinner_v[:, pl.ds(pl.multiple_of(offset, width), width)])
        value = value.astype(jnp.bfloat16)
        for half in range(2):
            row = (2 * part + half) * chunk
            ew_natural[:, row : row + chunk, :] = value[
                :, half * part_width : (half + 1) * part_width
            ].reshape(shards, chunk, part_width)
        rows_at = slice(2 * part * chunk, (2 * part + 2) * chunk)
        place_shards(me, ew_natural, ew_keep, ew_send, MASKS_B, 0, shards, rows_at)
    save.wait()


def feed_back(
    place, own, other, y, final_gain, dm, normed_two, biases, wc, slope, active, dinner, shards
):
    rows, width = own.shape
    count = 2 * rows
    hidden_width = wc.shape[0]
    parts = hidden_width // width
    low, full = jnp.bfloat16, jnp.float32
    height = hidden_width // shards
    half = jax.ShapeDtypeStruct((shards // 2, height, width // 2), low)
    bottom = pl.BlockSpec((rows, width), lambda i: (1, 0))
    return pl.pallas_call(
        feed_kernel,
        grid=(1,),
        in_specs=[scalars()]
        + [whole_vmem()] * 2
        + [bottom]
        + [whole_vmem()] * 5
        + [in_place()] * 4,
        out_specs=[whole_vmem()] * 5 + [in_place(), whole_vmem(), whole_vmem()],
        out_shape=[half] * 4
        + [
            jax.ShapeDtypeStruct((rows, width), full),
            jax.ShapeDtypeStruct((rows, hidden_width), low),
            jax.ShapeDtypeStruct((1, width), full),
            jax.ShapeDtypeStruct((1, hidden_width), full),
        ],
        scratch_shapes=[
            pltpu.VMEM(wc.shape, low),
            pltpu.VMEM((rows, hidden_width), low),
            pltpu.VMEM((count, hidden_width), low),
            pltpu.VMEM((count, hidden_width), low),
            pltpu.VMEM((count, width), low),
            pltpu.VMEM((shards, height, width // 2), low),
            pltpu.VMEM((shards, height, width // 2), low),
            pltpu.SemaphoreType.DMA((2, parts)),
            pltpu.SemaphoreType.DMA((1 + parts,)),
            pltpu.SemaphoreType.DMA((1,)),
        ],
        compiler_params=pltpu.CompilerParams(vmem_limit_bytes=34 << 20),
        cost_estimate=pl.CostEstimate(
            flops=12_000_000_000, bytes_accessed=1_000_000, transcendentals=0
        ),
        name="feed_back",
    )(
        place,
        own,
        other,
        *far(y, final_gain),
        dm,
        *far(normed_two),
        *biases,
        *far(wc, slope, active),
        dinner,
    )


def branch_kernel(
    place_ref,
    dy_ref,
    after_ref,
    mixed_ref,
    second_gain,
    dbranch_first,
    second_gain_first,
    second_shift_first,
    attend_bias_first,
    dinner_ref,
    we_hbm,
    wao_hbm,
    dafter_out,
    dmixed_out,
    attend_out,
    second_gain_out,
    second_shift_out,
    attend_bias_out,
    we,
    wao,
    dbranch_v,
    load_sem,
):
    blk = place_ref[1]
    loads = expand_loads(we_hbm, we, wao_hbm, wao, load_sem)
    for load in loads:
        load.start()
    rows, width = after_ref.shape
    part_width = width // 2
    dafter, gain_sum, shift_sum = branch_rows(
        dinner_ref, we, loads, after_ref, second_gain, dy_ref[...]
    )
    dafter_out[...] = dafter
    second_gain_out[...] = second_gain_first[...] + gain_sum
    second_shift_out[...] = second_shift_first[...] + shift_sum
    dbranch = dafter.astype(jnp.bfloat16)
    dbranch_v[:rows] = dbranch_first[...]
    dbranch_v[rows:] = dbranch
    attend_bias_out[...] = attend_bias_first[...] + row_sums(dbranch)
    loads[-1].wait()
    dmixed_out[...] = nt(dbranch, wao[...]).astype(jnp.bfloat16)
    part = dbranch_v[:, pl.ds(pl.multiple_of(blk * part_width, part_width), part_width)]
    attend_out[...] = tn(mixed_ref[...], part).astype(jnp.bfloat16).reshape(attend_out.shape)


def branch_back(place, dy, after, mixed, second_gain, dbranch, sums, dinner, we, wao, carry, shards):
    rows, width = dy.shape
    parts = we.shape[1] // width
    low, full = jnp.bfloat16, jnp.float32
    vector = jax.ShapeDtypeStruct((1, width), full)
    bottom = pl.BlockSpec((rows, width), lambda i: (1, 0))
    return pl.pallas_call(
        carrying(branch_kernel, 12, 6, len(carry)),
        grid=(1,),
        in_specs=[scalars(), whole_vmem(), bottom]
        + [whole_vmem()] * 7
        + [in_place()] * (2 + len(carry)),
        out_specs=[whole_vmem()] * 6 + [in_place()] * len(carry),
        input_output_aliases=aliases(12, 6, carry),
        out_shape=[
            jax.ShapeDtypeStruct((rows, width), full),
            jax.ShapeDtypeStruct((rows, width), low),
            jax.ShapeDtypeStruct((shards, width // shards, width // 2), low),
            vector,
            vector,
            vector,
        ]
        + shapes_of(carry),
        scratch_shapes=[
            pltpu.VMEM(we.shape, low),
            pltpu.VMEM(wao.shape, low),
            pltpu.VMEM((2 * rows, width), low),
            pltpu.SemaphoreType.DMA((parts + 1,)),
        ],
        compiler_params=pltpu.CompilerParams(vmem_limit_bytes=22 << 20),
        cost_estimate=pl.CostEstimate(
            flops=12_000_000_000, bytes_accessed=1_000_000, transcendentals=0
        ),
        name="branch_back",
    )(
        place,
        dy,
        *far(after, mixed, second_gain),
        dbranch,
        *sums,
        dinner,
        *far(we, wao),
        *carry,
    )


def attend_pair(block, query_ref, keys_ref, values_ref, probs_ref, dmixed_refs):
    count, pair = query_ref.shape
    query = query_ref[...] * jnp.bfloat16(0.125)
    zero = jnp.bfloat16(0.0)
    dkeys = jnp.zeros((count, pair), jnp.float32)
    dvalues = jnp.zeros((count, pair), jnp.float32)
    keys = keys_ref[...] * jnp.bfloat16(0.125)
    dqueries = []
    for piece in reversed(range(count // block)):
        span = slice(piece * block, (piece + 1) * block)
        reach = (piece + 1) * block
        dquery = jnp.zeros((block, pair), jnp.float32)
        add_keys = jnp.zeros((reach, pair), jnp.float32)
        add_values = jnp.zeros((reach, pair), jnp.float32)
        for which in range(2):
            mask = head_mask((block, pair), which)
            grad = jnp.where(mask, dmixed_refs[piece][...], zero)
            mine = jnp.where(mask, query[span], zero)
            probs = probs_ref[which, :reach, span]
            dprobs = nt(values_ref[:reach], grad)
            wide = probs.astype(jnp.float32)
            product = wide * dprobs
            balance = jnp.sum(product, axis=0, keepdims=True)
            dscores = (product - wide * balance).astype(jnp.bfloat16)
            add_values = add_values + dense(probs, grad)
            add_keys = add_keys + dense(dscores, mine)
            dquery = dquery + tn(
                dscores, jnp.where(head_mask((reach, pair), which), keys[:reach], zero)
            )
        dqueries.insert(0, dquery.astype(jnp.bfloat16))
        if reach < count:
            pad = jnp.zeros((count - reach, pair), jnp.float32)
            add_keys = jnp.concatenate([add_keys, pad], axis=0)
            add_values = jnp.concatenate([add_values, pad], axis=0)
        dkeys = dkeys + add_keys
        dvalues = dvalues + add_values
    return (
        jnp.concatenate(dqueries, axis=0),
        dkeys.astype(jnp.bfloat16),
        dvalues.astype(jnp.bfloat16),
    )


def attend_kernel(
    block,
    _,
    query_ref,
    keys_ref,
    values_ref,
    probs_ref,
    dmixed_first,
    dmixed_second,
    dq_ref,
    dk_ref,
    dv_ref,
):
    dmixed = (dmixed_first, dmixed_second)
    grads = attend_pair(block, query_ref, keys_ref, values_ref, probs_ref, dmixed)
    for ref, grad in zip((dq_ref, dk_ref, dv_ref), grads):
        ref[...] = grad


def project_kernel(
    block,
    place_ref,
    query_ref,
    keys_ref,
    values_ref,
    probs_ref,
    dmixed_first,
    dmixed_second,
    normed_ref,
    attend_ref,
    dq_ref,
    dk_ref,
    dv_ref,
    keep,
    send,
    natural,
):
    step = pl.program_id(0)
    pair = query_ref.shape[1]
    column = pl.ds(pl.multiple_of(step * pair, pair), pair)
    dmixed = (dmixed_first, dmixed_second)
    grads = attend_pair(block, query_ref, keys_ref, values_ref, probs_ref, dmixed)
    for ref, grad in zip((dq_ref, dk_ref, dv_ref), grads):
        ref[:, column] = grad

    @pl.when(step == pl.num_programs(0) - 1)
    def _():
        me = place_ref[0]
        shards = natural.shape[0]
        width = normed_ref.shape[1]
        part_width = width // 2
        chunk = width // shards
        natural[:, :chunk, :] = attend_ref[...]
        for part, ref in enumerate((dq_ref, dk_ref, dv_ref)):
            value = tn(normed_ref[...], ref[...]).astype(jnp.bfloat16)
            natural[:, (part + 1) * chunk : (part + 2) * chunk, :] = value.reshape(
                shards, chunk, part_width
            )
            rows = slice(0, 2 * chunk) if part == 0 else slice((part + 1) * chunk, (part + 2) * chunk)
            place_shards(me, natural, keep, send, MASKS, 0, shards, rows)


def attend_specs(joined, dmixed, own):
    rows, width = dmixed[0].shape
    count = 2 * rows
    pair = 2 * HEAD_DIM
    pairs = width // pair
    half = pairs // 2

    def first(place_ref):
        blk = place_ref[1]
        return half * (blk if own else 1 - blk)

    def column(height, offset):
        return pl.BlockSpec((height, pair), lambda p, place_ref: (0, offset + first(place_ref) + p))

    return half, [
        column(count, 0),
        column(count, pairs),
        column(count, 2 * pairs),
        pl.BlockSpec((2, count, count), lambda p, place_ref: (first(place_ref) + p, 0, 0)),
        column(rows, 0),
        column(rows, 0),
    ]


def attend_back(place, joined, probs, dmixed, carry, block):
    width = dmixed[0].shape[1]
    count = joined.shape[0]
    half, specs = attend_specs(joined, dmixed, False)
    result = pl.BlockSpec((count, 2 * HEAD_DIM), lambda p, place_ref: (0, p))
    return pl.pallas_call(
        carrying(functools.partial(attend_kernel, block), 7, 3, len(carry)),
        grid_spec=pltpu.PrefetchScalarGridSpec(
            num_scalar_prefetch=1,
            grid=(half,),
            in_specs=specs + [in_place()] * len(carry),
            out_specs=[result] * 3 + [in_place()] * len(carry),
        ),
        out_shape=[jax.ShapeDtypeStruct((count, width // 2), jnp.bfloat16)] * 3
        + shapes_of(carry),
        input_output_aliases=aliases(7, 3, carry),
        compiler_params=pltpu.CompilerParams(vmem_limit_bytes=16 << 20),
        cost_estimate=pl.CostEstimate(
            flops=12_000_000_000, bytes_accessed=1_000_000, transcendentals=0
        ),
        name="attend_back",
    )(place, *far(joined, joined, joined, probs), *dmixed, *carry)


def project_back(place, joined, probs, dmixed, normed, attend, carry, block, shards):
    count, width = normed.shape
    chunk = width // shards
    half, specs = attend_specs(joined, dmixed, True)
    result = pl.BlockSpec((count, width // 2), lambda p, place_ref: (0, 0))
    piece = jax.ShapeDtypeStruct((shards // 2, 4 * chunk, width // 2), jnp.bfloat16)
    specs = specs + [
        pl.BlockSpec(normed.shape, lambda p, place_ref: (0, 0)),
        pl.BlockSpec(attend.shape, lambda p, place_ref: (0, 0, 0)),
    ]
    return pl.pallas_call(
        carrying(functools.partial(project_kernel, block), 9, 5, len(carry)),
        grid_spec=pltpu.PrefetchScalarGridSpec(
            num_scalar_prefetch=1,
            grid=(half,),
            in_specs=specs + [in_place()] * len(carry),
            out_specs=[result] * 3 + [whole_vmem()] * 2 + [in_place()] * len(carry),
            scratch_shapes=[pltpu.VMEM((shards, 4 * chunk, width // 2), jnp.bfloat16)],
        ),
        out_shape=[jax.ShapeDtypeStruct((count, width // 2), jnp.bfloat16)] * 3
        + [piece, piece]
        + shapes_of(carry),
        input_output_aliases=aliases(9, 5, carry),
        compiler_params=pltpu.CompilerParams(vmem_limit_bytes=18 << 20),
        cost_estimate=pl.CostEstimate(
            flops=12_000_000_000, bytes_accessed=1_000_000, transcendentals=0
        ),
        name="project_back",
    )(place, *far(joined, joined, joined, probs), *dmixed, *far(normed), attend, *carry)


def input_kernel(
    place_ref,
    own_ref,
    other_ref,
    dq_own,
    dk_own,
    dv_own,
    dq_other,
    dk_other,
    dv_other,
    dafter_first,
    dafter_second,
    first_gain,
    attend_bias_grad,
    second_gain_grad,
    second_shift_grad,
    expand_bias_grad,
    contract_bias_grad,
    wpi_hbm,
    grad_out,
    keep,
    send,
    wpi,
    joined_v,
    x_v,
    grad_v,
    load_sem,
):
    me, blk = place_ref[0], place_ref[1]
    load = pltpu.make_async_copy(wpi_hbm, wpi, load_sem.at[0])
    load.start()
    count, width = x_v.shape
    part_width = width // 2
    shards = 2 * keep.shape[0]
    in_stream_order(x_v, own_ref, other_ref, blk)
    for side, group in ((blk, (dq_own, dk_own, dv_own)), (1 - blk, (dq_other, dk_other, dv_other))):
        for part, ref in enumerate(group):
            offset = part * width + side * part_width
            joined_v[:, pl.ds(pl.multiple_of(offset, part_width), part_width)] = ref[...]
    normed, scale = normalise(x_v[...])
    load.wait()
    dh1 = nt(joined_v[...], wpi[...])
    sums = jnp.sum(joined_v[...].astype(jnp.float32), axis=0, keepdims=True)
    vectors = [
        jnp.sum(dh1 * normed, axis=0, keepdims=True),
        jnp.sum(dh1, axis=0, keepdims=True),
        jnp.concatenate([sums[:, :width], sums[:, 2 * width :]], axis=1),
        attend_bias_grad[...],
        second_gain_grad[...],
        second_shift_grad[...],
        expand_bias_grad[...],
        contract_bias_grad[...],
    ]
    mine = lax.rem(me, 2)
    place = position(me, MASKS)
    for shard in range(shards):
        rows = []
        for vector in vectors:
            size = vector.shape[1] // shards
            piece = vector[:, shard * size : (shard + 1) * size]
            rows.append(jnp.concatenate([piece, jnp.zeros((1, 256 - size), jnp.float32)], axis=1))
        value = jnp.concatenate(rows, axis=0)
        target = lax.bitwise_xor(place, jnp.int32(position(shard, MASKS)))

        @pl.when(mine == shard % 2)
        def _():
            keep[target] = value

        @pl.when(mine != shard % 2)
        def _():
            send[target] = value

    rows = own_ref.shape[0]
    grad_v[...] = norm_back(normed, scale, as_row(first_gain), dh1)
    grad_v[:rows] += dafter_first[...]
    grad_v[rows:] += dafter_second[...]
    grad_out[...] = grad_v[pl.ds(pl.multiple_of(blk * rows, rows), rows), :]


def input_back(place, own, other, parts, dafter, gain, vectors, wpi, carry, shards):
    rows, width = own.shape
    count = 2 * rows
    low, full = jnp.bfloat16, jnp.float32
    half = jax.ShapeDtypeStruct((shards // 2, len(vectors) + 3, 256), full)
    return pl.pallas_call(
        carrying(input_kernel, 18, 3, len(carry)),
        in_specs=[scalars()] + [whole_vmem()] * 16 + [in_place()] * (1 + len(carry)),
        out_specs=[whole_vmem()] * 3 + [in_place()] * len(carry),
        out_shape=[jax.ShapeDtypeStruct((rows, width), full), half, half] + shapes_of(carry),
        input_output_aliases=aliases(18, 3, carry),
        scratch_shapes=[
            pltpu.VMEM(wpi.shape, low),
            pltpu.VMEM((count, 3 * width), low),
            pltpu.VMEM((count, width), full),
            pltpu.VMEM((count, width), full),
            pltpu.SemaphoreType.DMA((1,)),
        ],
        compiler_params=pltpu.CompilerParams(vmem_limit_bytes=24 << 20),
        cost_estimate=pl.CostEstimate(
            flops=12_000_000_000, bytes_accessed=1_000_000, transcendentals=0
        ),
        name="input_back",
    )(
        place, *far(own, other), *parts, *dafter, *far(gain), *vectors, *far(wpi), *carry
    )


def across(value, mask):
    return lax.ppermute(value, "dp", [(i, i ^ mask) for i in range(lax.axis_size("dp"))])


def halve(keep, received):
    half = keep.shape[0] // 2
    return (keep[:half] + received[:half], keep[half:] + received[half:])


def merge_kernel(layout, *refs):
    total = sum(1 + parts for parts in layout)
    inputs, outputs = list(refs[:total]), list(refs[total:])
    done = 0
    for parts in layout:
        keep = inputs.pop(0)
        half = keep.shape[0] // 2
        if half == 0:
            targets = [(outputs[-1].at[done : done + 1], slice(0, 1))]
            done += 1
        else:
            targets = [(outputs.pop(0), slice(0, half)), (outputs.pop(0), slice(half, 2 * half))]
        row = 0
        for _ in range(parts):
            got = inputs.pop(0)
            rows = slice(row, row + got.shape[1])
            row = rows.stop
            for target, which in targets:
                target[:, rows] = keep[which, rows] + got[which]


def merge(*pairs):
    shapes, finals = [], [pair[0] for pair in pairs if pair[0].shape[0] == 1]
    for keep, *_ in pairs:
        if keep.shape[0] > 1:
            shapes += [jax.ShapeDtypeStruct((keep.shape[0] // 2, *keep.shape[1:]), keep.dtype)] * 2
    if finals:
        shapes.append(jax.ShapeDtypeStruct((len(finals), *finals[0].shape[1:]), finals[0].dtype))
    arrays = [array for pair in pairs for array in pair]
    return pl.pallas_call(
        functools.partial(merge_kernel, [len(pair) - 1 for pair in pairs]),
        in_specs=[whole_vmem()] * len(arrays),
        out_specs=[whole_vmem()] * len(shapes),
        out_shape=shapes,
        compiler_params=pltpu.CompilerParams(vmem_limit_bytes=16 << 20),
        cost_estimate=pl.CostEstimate(flops=1_000_000, bytes_accessed=1_000_000, transcendentals=0),
        name="merge",
    )(*arrays)


def swap(value):
    return lax.ppermute(value, "blk", [(0, 1), (1, 0)])


def both_halves(own, other, blk):
    return jnp.where(
        blk == 0,
        jnp.concatenate([own, other], axis=-1),
        jnp.concatenate([other, own], axis=-1),
    ).astype(jnp.float32)


def local_pair(hidden, doc_lengths, *arrays):
    student, teacher = arrays[:12], arrays[12:24]
    final_gain, final_shift, table = arrays[24:]
    rows, width = hidden.shape
    shards = lax.axis_size("dp")
    blk = lax.axis_index("blk")
    place = jnp.stack([lax.axis_index("dp"), blk]).astype(jnp.int32)
    other = swap(hidden)
    def block(train, params):
        gain, shift, wpi, qvb, wao, bao, gain_two, shift_two, we, be, wc, bc = params
        vectors = (gain, shift, qvb, bao, gain_two, shift_two, be, bc, final_gain, final_shift)
        return forward(
            train,
            place,
            doc_lengths,
            hidden,
            other,
            vectors,
            (wpi, wao, we, wc),
        )

    (rows_t,) = block(False, teacher)
    rows_s, normed, joined, probs, mixed, after, normed_two, slope, active, y = block(True, student)
    diff, expo, stats, sums = logits_phase(rows_s, rows_t, table)
    gain, shift, wpi, qvb, wao, bao, gain_two, shift_two, we, be, wc, bc = student
    sums_other = swap(sums)
    own_first, low_first, kl_first = gradient_phase(diff, expo, table, stats, sums, sums_other, 0)
    got_first = swap(low_first)
    own_second, low_second, kl_second = gradient_phase(
        diff, expo, table, stats, sums, sums_other, 1
    )
    got_second = swap(low_second)
    dm, dinner, dafter_first, dbranch, dmixed_first, dbc, dbe, *branch_sums = first_rows(
        own_first, got_first, y, after, final_gain, gain_two, wc, we, wao, slope
    )
    cw_keep, cw_send, ew_keep, ew_send, dy, dinner, dbc, dbe = feed_back(
        place,
        own_second,
        got_second,
        y,
        final_gain,
        dm,
        normed_two,
        (dbc, dbe),
        wc,
        slope,
        active,
        dinner,
        shards,
    )
    cw_got = across(cw_send, MASKS[0])
    ew_got = across(ew_send, MASKS_B[0])
    dafter_second, dmixed_second, attend, dgain_two, dshift_two, dbao, cw_keep, ew_keep = (
        branch_back(
            place,
            dy,
            after,
            mixed,
            gain_two,
            dbranch,
            branch_sums,
            dinner,
            we,
            wao,
            (cw_keep, ew_keep),
            shards,
        )
    )
    dafter, dmixed = (dafter_first, dafter_second), (dmixed_first, dmixed_second)
    cw_keep, cw_send = halve(cw_keep, cw_got)
    cw_got = across(cw_send, MASKS[1])
    ew_keep, ew_send = halve(ew_keep, ew_got)
    ew_got = across(ew_send, MASKS_B[1])
    *own_grads, keep, send, cw_keep, ew_keep = project_back(
        place, joined, probs, dmixed, normed, attend, (cw_keep, ew_keep), rows, shards
    )
    got = across(send, MASKS[0])
    cw_keep, cw_send, ew_keep, ew_send = merge((cw_keep, cw_got), (ew_keep, ew_got))
    cw_got = across(cw_send, MASKS[2])
    ew_got = across(ew_send, MASKS_B[2])
    *other_grads, keep, cw_keep, ew_keep = attend_back(
        place, joined, probs, dmixed, (keep, cw_keep, ew_keep), rows
    )
    keep, send, cw_keep, cw_send, ew_keep, ew_send = merge(
        (keep, got), (cw_keep, cw_got), (ew_keep, ew_got)
    )
    got = across(send, MASKS[1])
    cw_got = across(cw_send, MASKS[3])
    ew_got = across(ew_send, MASKS_B[3])
    input_grad, vector_keep, vector_send, keep, cw_keep, ew_keep = input_back(
        place,
        hidden,
        other,
        (*own_grads, *other_grads),
        dafter,
        gain,
        (dbao, dgain_two, dshift_two, dbe, dbc),
        wpi,
        (keep, cw_keep, ew_keep),
        shards,
    )
    vector_got = across(vector_send, MASKS[0])
    keep, send, vector_keep, vector_send, both = merge(
        (keep, got), (cw_keep, cw_got), (ew_keep, ew_got), (vector_keep, vector_got)
    )
    got, both_other = across(send, MASKS[2]), swap(both)
    vector_got = across(vector_send, MASKS[1])
    keep, send, vector_keep, vector_send = merge((keep, got), (vector_keep, vector_got))
    got, vector_got = across(send, MASKS[3]), across(vector_send, MASKS[2])
    vector_keep, vector_send, last = merge((keep, got), (vector_keep, vector_got))
    last = last[0]
    last_other = swap(last)
    vectors = (vector_keep + across(vector_send, MASKS[3]))[0]
    cw, ew, cw_other, ew_other = both[0], both[1], both_other[0], both_other[1]
    chunk = width // shards

    def wide(own, other):
        own, other = (part.reshape(-1, chunk, part.shape[1]) for part in (own, other))
        order = [own[i] for i in range(own.shape[0])], [other[i] for i in range(own.shape[0])]
        return order

    grad_cw = both_halves(cw, cw_other, blk)
    own, other = wide(ew, ew_other)
    grad_ew = both_halves(jnp.concatenate(own, axis=1), jnp.concatenate(other, axis=1), blk)
    own, other = wide(last, last_other)
    grad_ao = both_halves(own[0], other[0], blk)
    grad_pi = jnp.concatenate([both_halves(own[i], other[i], blk) for i in (1, 2, 3)], axis=1)
    sizes = (chunk, chunk, 2 * chunk, chunk, chunk, chunk, be.shape[0] // shards, chunk)
    dgain, dshift, dqvb, dbao, dgain_two, dshift_two, dbe, dbc = (
        vectors[index, :size] for index, size in enumerate(sizes)
    )
    return (
        jnp.where(blk == 0, kl_first[0], kl_second[0]),
        input_grad,
        dgain,
        dshift,
        grad_pi,
        dqvb,
        grad_ao,
        dbao,
        dgain_two,
        dshift_two,
        grad_ew,
        dbe,
        grad_cw,
        dbc,
    )


def solution(mesh):
    pair = mesh.shape["dp"] == 16 and mesh.shape["blk"] == 2
    return jax.shard_map(
        local_pair if pair else local_general,
        mesh=mesh,
        in_specs=(
            P(("dp", "blk"), None),
            P("dp", None),
            P(),
            P(),
            P(),
            P(),
            P(),
            P(),
            P(),
            P(),
            P(),
            P(),
            P(),
            P(),
            P(),
            P(),
            P(),
            P(),
            P(),
            P(),
            P(),
            P(),
            P(),
            P(),
            P(),
            P(),
            P(),
            P(),
            P("blk", None),
        ),
        out_specs=(
            P(("dp", "blk")),
            P(("dp", "blk"), None),
            P("dp"),
            P("dp"),
            P("dp", None),
            P("dp"),
            P("dp", None),
            P("dp"),
            P("dp"),
            P("dp"),
            P("dp", None),
            P("dp"),
            P("dp", None),
            P("dp"),
        ),
        check_vma=False,
    )
```

profile of v0, /device:TPU:0, one launch (start us, length us, event | category | flops | bytes accessed | tf_op | source)
XLA Modules:
  0.0 230.6 jit_solution(2722400201188730162)
XLA Ops:
  0.6 3.0 %collective-permute-start = (bf16[256,768]{1,0:T(8,128)(2,1)}, bf16[256,768]{1,0:T(8,128)(2,1)S(1)}, u32[]{:S(2)}, u32[]{:S(2)}) collective-permute-start(bf16[256,768]{1,0:T(8,128)(2,1)} %refs_1_.5), channel_id=1, source_target_pairs={{0,1},{1,0},{2,3},{3,2},{4,5},{5,4},{6,7},{7,6},{8,9},{9,8},{10,11... | collective-permute-start | bytes 1179656 | tf_op jit(solution)/shard_map/ppermute | solution.py:1684
  3.8 9.2 %collective-permute-done.refs_3_.refs_2_ = bf16[256,768]{1,0:T(8,128)(2,1)S(1)} collective-permute-done((bf16[256,768]{1,0:T(8,128)(2,1)}, bf16[256,768]{1,0:T(8,128)(2,1)S(1)}, u32[]{:S(2)}, u32[]{:S(2)}) %collective-permute-start) | collective-permute-done | bytes 393248 | tf_op jit(solution)/shard_map/ppermute | solution.py:1684
  14.7 18.4 %forward_teacher.1.teacher_ref = bf16[512,768]{1,0:T(8,128)(2,1)S(1)} custom-call(s32[2]{0:T(128)S(1)} %pad_add_fusion.refs_0_.place_ref, s32[1,4]{1,0:T(1,128)S(1)} %copy-done.2, bf16[256,768]{1,0:T(8,128)(2,1)S(1)} %copy-done, bf16[256,768]{1,0:T(8,128)(2,1)S(1)} %collective-permute-done.refs_3_.refs_2_, f32[768]{0:T(1024)} %refs_4_.4, f32[768]{0:T(1024)} %refs_5_.3, ...), custom_call_target="tpu_custom_call" | custom-call | flops 8000000000 | bytes 20000000 | tf_op jit(solution)/shard_map/forward_teacher/pallas_call | solution.py:729
  33.1 22.0 %forward_student.1 = (bf16[512,768]{1,0:T(8,128)(2,1)}, bf16[512,768]{1,0:T(8,128)(2,1)}, bf16[512,2304]{1,0:T(8,128)(2,1)}, bf16[12,512,512]{2,1,0:T(8,128)(2,1...) custom-call(s32[2]{0:T(128)} %copy-done.3, ...), custom_call_target="tpu_custom_call" | custom-call | flops 8000000000 | bytes 20000000 | tf_op jit(solution)/shard_map/forward_student/pallas_call | solution.py:729
  56.3 40.9 %logits_phase.1 = (bf16[512,16384]{1,0:T(8,128)(2,1)S(1)}, bf16[512,16384]{1,0:T(8,128)(2,1)}, f32[8,40,512]{2,1,0:T(8,128)S(1)}, f32[8,512]{1,0:T(8,128)S(1)}) custom-call(bf16[512,768]{1,0:T(8,128)(2,1)S(1)} %copy-done.5, bf16[512,768]{1,0:T(8,128)(2,1)S(1)} %forward_teacher.1.teacher_ref, bf16[16384,768]{1,0:T(8,128)(2,1)} %table_ref.5), custom_call_target="tpu_custom_call" | custom-call | flops 25769803776 | bytes 60000000 | tf_op jit(solution)/shard_map/logits_phase/pallas_call | solution.py:802
  97.2 1.7 collective-permute-start.1
  98.9 2.0 collective-permute-done.1.other_ref
  101.0 16.5 %gradient_first.1 = (f32[256,768]{1,0:T(8,128)S(1)}, bf16[256,768]{1,0:T(8,128)(2,1)S(1)}, f32[1,256]{1,0:T(1,128)S(1)}) custom-call(bf16[512,16384]{1,0:T(8,128)(2,1)S(1)} %get-tuple-element.102.diff_ref, bf16[512,16384]{1,0:T(8,128)(2,1)} %get-tuple-element.103.expo_ref, bf16[16384,768]{1,0:T(8,128)(2,1)} %table_ref.5, ...), custom_call_target="tpu_custom_call" | custom-call | flops 12884901888 | bytes 60000000 | tf_op jit(solution)/shard_map/gradient_first/pallas_call | solution.py:896
  117.5 1.8 collective-permute-start.2
  119.3 16.6 %gradient_second.1 = (f32[256,768]{1,0:T(8,128)S(1)}, bf16[256,768]{1,0:T(8,128)(2,1)S(1)}, f32[1,256]{1,0:T(1,128)S(1)}) custom-call(bf16[512,16384]{1,0:T(8,128)(2,1)S(1)} %get-tuple-element.102.diff_ref, bf16[512,16384]{1,0:T(8,128)(2,1)} %get-tuple-element.103.expo_ref, bf16[16384,768]{1,0:T(8,128)(2,1)} %table_ref.5, ...), custom_call_target="tpu_custom_call" | custom-call | flops 12884901888 | bytes 60000000 | tf_op jit(solution)/shard_map/gradient_second/pallas_call | solution.py:896
  136.2 9.6 %first_rows.1 = (bf16[256,768]{1,0:T(8,128)(2,1)S(1)}, bf16[256,3072]{1,0:T(8,128)(2,1)S(1)}, f32[256,768]{1,0:T(8,128)S(1)}, bf16[256,768]{1,0:T(8,128)(2,1)S(1...) custom-call(f32[256,768]{1,0:T(8,128)S(1)} %get-tuple-element.110.ow, ...), custom_call_target="tpu_custom_call" | custom-call | flops 12000000000 | bytes 1000000 | tf_op jit(solution)/shard_map/first_rows/pallas_call | solution.py:1070
  145.8 11.0 %feed_back.1 = (bf16[8,192,384]{2,1,0:T(8,128)(2,1)S(1)}, bf16[8,192,384]{2,1,0:T(8,128)(2,1)S(1)}, bf16[8,192,384]{2,1,0:T(8,128)(2,1)S(1)}, bf16[8,192,384]{2,...) custom-call(s32[2]{0:T(128)S(1)} %copy-done.4, ...), custom_call_target="tpu_custom_call" | custom-call | flops 12000000000 | bytes 1000000 | tf_op jit(solution)/shard_map/feed_back/pallas_call | solution.py:1205
  157.4 6.7 %branch_back.1 = (f32[256,768]{1,0:T(8,128)S(1)}, bf16[256,768]{1,0:T(8,128)(2,1)S(1)}, bf16[16,48,384]{2,1,0:T(8,128)(2,1)S(1)}, f32[1,768]{1,0:T(1,128)S(1)}, ...) custom-call(s32[2]{0:T(128)S(1)} %copy-done.4, ...), custom_call_target="tpu_custom_call", output_to_operand_aliasing={{6}: (12, {}), {7}: (13, {})} | custom-call | flops 12000000000 | bytes 1000000 | tf_op jit(solution)/shard_map/branch_back/pallas_call | solution.py:1303
  164.3 1.8 collective-permute-start.6
  166.3 1.6 collective-permute-start.7
  167.9 8.7 %project_back.1 = (bf16[512,384]{1,0:T(8,128)(2,1)S(1)}, bf16[512,384]{1,0:T(8,128)(2,1)S(1)}, bf16[512,384]{1,0:T(8,128)(2,1)S(1)}, bf16[8,192,384]{2,1,0:T(8,1...) custom-call(s32[2]{0:T(128)S(1)} %copy-done.4, ...), custom_call_target="tpu_custom_call", output_to_operand_aliasing={{5}: (9, {}), {6}: (10, {})} | custom-call | flops 12000000000 | bytes 1000000 | tf_op jit(solution)/shard_map/project_back/pallas_call | solution.py:1506
  176.7 3.0 %collective-permute-done.6.refs_1_ = bf16[4,192,384]{2,1,0:T(8,128)(2,1)S(1)} collective-permute-done((bf16[4,192,384]{2,1,0:T(8,128)(2,1)S(1)}, bf16[4,192,384]{2,1,0:T(8,128)(2,1)S(1)}, u32[]{:S(2)}, u32[]{:S(2)}) %collective-permute-start.6) | collective-permute-done | bytes 589856 | tf_op jit(solution)/shard_map/ppermute | solution.py:1635
  183.7 6.3 %attend_back.1 = (bf16[512,384]{1,0:T(8,128)(2,1)S(1)}, bf16[512,384]{1,0:T(8,128)(2,1)S(1)}, bf16[512,384]{1,0:T(8,128)(2,1)S(1)}, bf16[8,192,384]{2,1,0:T(8,12...) custom-call(s32[2]{0:T(128)S(1)} %copy-done.4, ...), custom_call_target="tpu_custom_call", output_to_operand_aliasing={{3}: (7, {}), {4}: (8, {}), {5}: (9, {})} | custom-call | flops 12000000000 | bytes 1000000 | tf_op jit(solution)/shard_map/attend_back/pallas_call | solution.py:1477
  191.0 2.7 %collective-permute-start.12 = (bf16[1,192,384]{2,1,0:T(8,128)(2,1)S(1)}, bf16[1,192,384]{2,1,0:T(8,128)(2,1)S(1)}, u32[]{:S(2)}, u32[]{:S(2)}) collective-permute-start(bf16[1,192,384]{2,1,0:T(8,128)(2,1)S(1)} %get-tuple-element.171), channel_id=1, source_target_pairs={{0,16},{2,18},{4,20},{6,22},{8,24},{10,26},{12,28},{14,30},{16,0},... | collective-permute-start | bytes 442376 | tf_op jit(solution)/shard_map/ppermute | solution.py:1635
  194.8 8.2 %input_back.1 = (f32[256,768]{1,0:T(8,128)}, f32[8,8,256]{2,1,0:T(8,128)S(1)}, f32[8,8,256]{2,1,0:T(8,128)S(1)}, bf16[4,192,384]{2,1,0:T(8,128)(2,1)S(1)}, bf16[...) custom-call(s32[2]{0:T(128)S(1)} %copy-done.4, ...), custom_call_target="tpu_custom_call", output_to_operand_aliasing={{3}: (18, {}), {4}: (19, {}), {5}: (20, {})} | custom-call | flops 12000000000 | bytes 1000000 | tf_op jit(solution)/shard_map/input_back/pallas_call | solution.py:1611
  210.6 2.6 %collective-permute-done.16.refs_3_ = f32[4,8,256]{2,1,0:T(8,128)S(1)} collective-permute-done((f32[4,8,256]{2,1,0:T(8,128)S(1)}, f32[4,8,256]{2,1,0:T(8,128)S(1)}, u32[]{:S(2)}, u32[]{:S(2)}) %collective-permute-start.16) | collective-permute-done | bytes 32800 | tf_op jit(solution)/shard_map/ppermute | solution.py:1635
  214.8 2.6 %collective-permute-start.17 = (bf16[1,192,384]{2,1,0:T(8,128)(2,1)S(1)}, bf16[1,192,384]{2,1,0:T(8,128)(2,1)S(1)}, u32[]{:S(2)}, u32[]{:S(2)}) collective-permute-start(bf16[1,192,384]{2,1,0:T(8,128)(2,1)S(1)} %get-tuple-element.181), channel_id=1, source_target_pairs={{0,16},{2,18},{4,20},{6,22},{8,24},{10,26},{12,28},{14,30},{16,0},... | collective-permute-start | bytes 442376 | tf_op jit(solution)/shard_map/ppermute | solution.py:1635
  219.3 3.2 %collective-permute-done.17.refs_1_ = bf16[1,192,384]{2,1,0:T(8,128)(2,1)S(1)} collective-permute-done((bf16[1,192,384]{2,1,0:T(8,128)(2,1)S(1)}, bf16[1,192,384]{2,1,0:T(8,128)(2,1)S(1)}, u32[]{:S(2)}, u32[]{:S(2)}) %collective-permute-start.17) | collective-permute-done | bytes 147488 | tf_op jit(solution)/shard_map/ppermute | solution.py:1635
  224.9 2.4 %collective-permute-done.19 = f32[1,8,256]{2,1,0:T(8,128)S(1)} collective-permute-done((f32[1,8,256]{2,1,0:T(8,128)S(1)}, f32[1,8,256]{2,1,0:T(8,128)S(1)}, u32[]{:S(2)}, u32[]{:S(2)}) %collective-permute-start.19) | collective-permute-done | bytes 8224 | tf_op jit(solution)/shard_map/ppermute | solution.py:1635
  (77 shorter events, 26.9 us)
Async XLA Ops:
  0.6 12.4 %collective-permute-start = (bf16[256,768]{1,0:T(8,128)(2,1)}, bf16[256,768]{1,0:T(8,128)(2,1)S(1)}, u32[]{:S(2)}, u32[]{:S(2)}) collective-permute-start(bf16[256,768]{1,0:T(8,128)(2,1)} %refs_1_.5), channel_id=1, source_target_pairs={{0,1},{1,0},{2,3},{3,2},{4,5},{5,4},{6,7},{7,6},{8,9},{9,8},{10,11... | collective-permute-start | bytes 1179656 | tf_op jit(solution)/shard_map/ppermute | solution.py:1684
  3.8 29.4 %copy-start.3 = (s32[2]{0:T(128)}, s32[2]{0:T(128)S(1)}, u32[]{:S(2)}) copy-start(s32[2]{0:T(128)S(1)} %pad_add_fusion.refs_0_.place_ref) | copy-start | bytes 28
  14.7 18.5 %copy-start.1 = (bf16[256,768]{1,0:T(8,128)(2,1)}, bf16[256,768]{1,0:T(8,128)(2,1)S(1)}, u32[]{:S(2)}) copy-start(bf16[256,768]{1,0:T(8,128)(2,1)S(1)} %collective-permute-done.refs_3_.refs_2_) | copy-start | bytes 1179652
  97.2 3.7 %collective-permute-start.1 = (f32[8,512]{1,0:T(8,128)S(1)}, f32[8,512]{1,0:T(8,128)S(1)}, u32[]{:S(2)}, u32[]{:S(2)}) collective-permute-start(f32[8,512]{1,0:T(8,128)S(1)} %get-tuple-element.105.own_ref), channel_id=1, source_target_pairs={{0,1},{1,0},{2,3},{3,2},{4,5},{5,4},{6,7},{7,6},{8,9},{9,8},{10,11... | collective-permute-start | bytes 49160 | tf_op jit(solution)/shard_map/ppermute | solution.py:1684
  117.5 18.7 %collective-permute-start.2 = (bf16[256,768]{1,0:T(8,128)(2,1)S(1)}, bf16[256,768]{1,0:T(8,128)(2,1)S(1)}, u32[]{:S(2)}, u32[]{:S(2)}) collective-permute-start(bf16[256,768]{1,0:T(8,128)(2,1)S(1)} %get-tuple-element.111), channel_id=1, source_target_pairs={{0,1},{1,0},{2,3},{3,2},{4,5},{5,4},{6,7},{7,6},{8,9},{9,8},{10,11... | collective-permute-start | bytes 1179656 | tf_op jit(solution)/shard_map/ppermute | solution.py:1684
  135.9 9.9 %collective-permute-start.3 = (bf16[256,768]{1,0:T(8,128)(2,1)S(1)}, bf16[256,768]{1,0:T(8,128)(2,1)S(1)}, u32[]{:S(2)}, u32[]{:S(2)}) collective-permute-start(bf16[256,768]{1,0:T(8,128)(2,1)S(1)} %get-tuple-element.117), channel_id=1, source_target_pairs={{0,1},{1,0},{2,3},{3,2},{4,5},{5,4},{6,7},{7,6},{8,9},{9,8},{10,11... | collective-permute-start | bytes 1179656 | tf_op jit(solution)/shard_map/ppermute | solution.py:1684
  156.9 7.3 %collective-permute-start.4 = (bf16[8,192,384]{2,1,0:T(8,128)(2,1)S(1)}, bf16[8,192,384]{2,1,0:T(8,128)(2,1)S(1)}, u32[]{:S(2)}, u32[]{:S(2)}) collective-permute-start(bf16[8,192,384]{2,1,0:T(8,128)(2,1)S(1)} %get-tuple-element.137), channel_id=1, source_target_pairs={{0,2},{2,0},{4,6},{6,4},{8,10},{10,8},{12,14},{14,12},{16,18},{18,... | collective-permute-start | bytes 3538952 | tf_op jit(solution)/shard_map/ppermute | solution.py:1635
  156.9 9.2 %collective-permute-start.5 = (bf16[8,192,384]{2,1,0:T(8,128)(2,1)S(1)}, bf16[8,192,384]{2,1,0:T(8,128)(2,1)S(1)}, u32[]{:S(2)}, u32[]{:S(2)}) collective-permute-start(bf16[8,192,384]{2,1,0:T(8,128)(2,1)S(1)} %get-tuple-element.139), channel_id=1, source_target_pairs={{0,2},{2,0},{4,6},{6,4},{8,10},{10,8},{12,14},{14,12},{16,18},{18,... | collective-permute-start | bytes 3538952 | tf_op jit(solution)/shard_map/ppermute | solution.py:1635
  164.3 15.4 %collective-permute-start.6 = (bf16[4,192,384]{2,1,0:T(8,128)(2,1)S(1)}, bf16[4,192,384]{2,1,0:T(8,128)(2,1)S(1)}, u32[]{:S(2)}, u32[]{:S(2)}) collective-permute-start(bf16[4,192,384]{2,1,0:T(8,128)(2,1)S(1)} %get-tuple-element.190), channel_id=1, source_target_pairs={{0,4},{2,6},{4,0},{6,2},{8,12},{10,14},{12,8},{14,10},{16,20},{18,... | collective-permute-start | bytes 1769480 | tf_op jit(solution)/shard_map/ppermute | solution.py:1635
  166.3 15.1 %collective-permute-start.7 = (bf16[4,192,384]{2,1,0:T(8,128)(2,1)S(1)}, bf16[4,192,384]{2,1,0:T(8,128)(2,1)S(1)}, u32[]{:S(2)}, u32[]{:S(2)}) collective-permute-start(bf16[4,192,384]{2,1,0:T(8,128)(2,1)S(1)} %get-tuple-element.188), channel_id=1, source_target_pairs={{0,8},{2,10},{4,12},{6,14},{8,0},{10,2},{12,4},{14,6},{16,24},{18,... | collective-permute-start | bytes 1769480 | tf_op jit(solution)/shard_map/ppermute | solution.py:1635
  176.6 14.1 %collective-permute-start.8 = (bf16[8,192,384]{2,1,0:T(8,128)(2,1)S(1)}, bf16[8,192,384]{2,1,0:T(8,128)(2,1)S(1)}, u32[]{:S(2)}, u32[]{:S(2)}) collective-permute-start(bf16[8,192,384]{2,1,0:T(8,128)(2,1)S(1)} %get-tuple-element.159), channel_id=1, source_target_pairs={{0,2},{2,0},{4,6},{6,4},{8,10},{10,8},{12,14},{14,12},{16,18},{18,... | collective-permute-start | bytes 3538952 | tf_op jit(solution)/shard_map/ppermute | solution.py:1635
  181.5 8.5 %collective-permute-start.9 = (bf16[2,192,384]{2,1,0:T(8,128)(2,1)S(1)}, bf16[2,192,384]{2,1,0:T(8,128)(2,1)S(1)}, u32[]{:S(2)}, u32[]{:S(2)}) collective-permute-start(bf16[2,192,384]{2,1,0:T(8,128)(2,1)S(1)} %get-tuple-element.161), channel_id=1, source_target_pairs={{0,8},{2,10},{4,12},{6,14},{8,0},{10,2},{12,4},{14,6},{16,24},{18,... | collective-permute-start | bytes 884744 | tf_op jit(solution)/shard_map/ppermute | solution.py:1635
  183.2 7.5 %collective-permute-start.10 = (bf16[2,192,384]{2,1,0:T(8,128)(2,1)S(1)}, bf16[2,192,384]{2,1,0:T(8,128)(2,1)S(1)}, u32[]{:S(2)}, u32[]{:S(2)}) collective-permute-start(bf16[2,192,384]{2,1,0:T(8,128)(2,1)S(1)} %get-tuple-element.163), channel_id=1, source_target_pairs={{0,4},{2,6},{4,0},{6,2},{8,12},{10,14},{12,8},{14,10},{16,20},{18,... | collective-permute-start | bytes 884744 | tf_op jit(solution)/shard_map/ppermute | solution.py:1635
  191.0 13.3 %collective-permute-start.12 = (bf16[1,192,384]{2,1,0:T(8,128)(2,1)S(1)}, bf16[1,192,384]{2,1,0:T(8,128)(2,1)S(1)}, u32[]{:S(2)}, u32[]{:S(2)}) collective-permute-start(bf16[1,192,384]{2,1,0:T(8,128)(2,1)S(1)} %get-tuple-element.171), channel_id=1, source_target_pairs={{0,16},{2,18},{4,20},{6,22},{8,24},{10,26},{12,28},{14,30},{16,0},... | collective-permute-start | bytes 442376 | tf_op jit(solution)/shard_map/ppermute | solution.py:1635
  193.7 11.2 %collective-permute-start.13 = (bf16[1,192,384]{2,1,0:T(8,128)(2,1)S(1)}, bf16[1,192,384]{2,1,0:T(8,128)(2,1)S(1)}, u32[]{:S(2)}, u32[]{:S(2)}) collective-permute-start(bf16[1,192,384]{2,1,0:T(8,128)(2,1)S(1)} %get-tuple-element.173), channel_id=1, source_target_pairs={{0,16},{2,18},{4,20},{6,22},{8,24},{10,26},{12,28},{14,30},{16,0},... | collective-permute-start | bytes 442376 | tf_op jit(solution)/shard_map/ppermute | solution.py:1635
  194.0 12.4 %collective-permute-start.11 = (bf16[4,192,384]{2,1,0:T(8,128)(2,1)S(1)}, bf16[4,192,384]{2,1,0:T(8,128)(2,1)S(1)}, u32[]{:S(2)}, u32[]{:S(2)}) collective-permute-start(bf16[4,192,384]{2,1,0:T(8,128)(2,1)S(1)} %get-tuple-element.169), channel_id=1, source_target_pairs={{0,4},{2,6},{4,0},{6,2},{8,12},{10,14},{12,8},{14,10},{16,20},{18,... | collective-permute-start | bytes 1769480 | tf_op jit(solution)/shard_map/ppermute | solution.py:1635
  203.0 1.3 collective-permute-start.14
  206.6 7.1 %collective-permute-start.15 = (bf16[2,192,384]{2,1,0:T(8,128)(2,1)S(1)}, bf16[2,192,384]{2,1,0:T(8,128)(2,1)S(1)}, u32[]{:S(2)}, u32[]{:S(2)}) collective-permute-start(bf16[2,192,384]{2,1,0:T(8,128)(2,1)S(1)} %get-tuple-element.177), channel_id=1, source_target_pairs={{0,8},{2,10},{4,12},{6,14},{8,0},{10,2},{12,4},{14,6},{16,24},{18,... | collective-permute-start | bytes 884744 | tf_op jit(solution)/shard_map/ppermute | solution.py:1635
  207.2 10.2 %collective-permute-start.21 = (bf16[2,192,384]{2,1,0:T(8,128)(2,1)S(1)}, bf16[2,192,384]{2,1,0:T(8,128)(2,1)S(1)}, u32[]{:S(2)}, u32[]{:S(2)}) collective-permute-start(bf16[2,192,384]{2,1,0:T(8,128)(2,1)S(1)} %get-tuple-element.187), channel_id=1, source_target_pairs={{0,1},{1,0},{2,3},{3,2},{4,5},{5,4},{6,7},{7,6},{8,9},{9,8},{10,11... | collective-permute-start | bytes 884744 | tf_op jit(solution)/shard_map/ppermute | solution.py:1684
  209.3 3.9 %collective-permute-start.16 = (f32[4,8,256]{2,1,0:T(8,128)S(1)}, f32[4,8,256]{2,1,0:T(8,128)S(1)}, u32[]{:S(2)}, u32[]{:S(2)}) collective-permute-start(f32[4,8,256]{2,1,0:T(8,128)S(1)} %get-tuple-element.179), channel_id=1, source_target_pairs={{0,4},{2,6},{4,0},{6,2},{8,12},{10,14},{12,8},{14,10},{16,20},{18,... | collective-permute-start | bytes 98312 | tf_op jit(solution)/shard_map/ppermute | solution.py:1635
  213.7 5.6 %collective-permute-start.18 = (f32[2,8,256]{2,1,0:T(8,128)S(1)}, f32[2,8,256]{2,1,0:T(8,128)S(1)}, u32[]{:S(2)}, u32[]{:S(2)}) collective-permute-start(f32[2,8,256]{2,1,0:T(8,128)S(1)} %get-tuple-element.183), channel_id=1, source_target_pairs={{0,8},{2,10},{4,12},{6,14},{8,0},{10,2},{12,4},{14,6},{16,24},{18,... | collective-permute-start | bytes 49160 | tf_op jit(solution)/shard_map/ppermute | solution.py:1635
  214.8 7.8 %collective-permute-start.17 = (bf16[1,192,384]{2,1,0:T(8,128)(2,1)S(1)}, bf16[1,192,384]{2,1,0:T(8,128)(2,1)S(1)}, u32[]{:S(2)}, u32[]{:S(2)}) collective-permute-start(bf16[1,192,384]{2,1,0:T(8,128)(2,1)S(1)} %get-tuple-element.181), channel_id=1, source_target_pairs={{0,16},{2,18},{4,20},{6,22},{8,24},{10,26},{12,28},{14,30},{16,0},... | collective-permute-start | bytes 442376 | tf_op jit(solution)/shard_map/ppermute | solution.py:1635
  222.6 4.6 %collective-permute-start.19 = (f32[1,8,256]{2,1,0:T(8,128)S(1)}, f32[1,8,256]{2,1,0:T(8,128)S(1)}, u32[]{:S(2)}, u32[]{:S(2)}) collective-permute-start(f32[1,8,256]{2,1,0:T(8,128)S(1)} %get-tuple-element.185), channel_id=1, source_target_pairs={{0,16},{2,18},{4,20},{6,22},{8,24},{10,26},{12,28},{14,30},{16,0},... | collective-permute-start | bytes 24584 | tf_op jit(solution)/shard_map/ppermute | solution.py:1635
  223.7 5.2 %collective-permute-start.20 = (bf16[192,384]{1,0:T(8,128)(2,1)S(1)}, bf16[192,384]{1,0:T(8,128)(2,1)S(1)}, u32[]{:S(2)}, u32[]{:S(2)}) collective-permute-start(bf16[192,384]{1,0:T(8,128)(2,1)S(1)} %bitcast.69), channel_id=1, source_target_pairs={{0,1},{1,0},{2,3},{3,2},{4,5},{5,4},{6,7},{7,6},{8,9},{9,8},{10,11... | collective-permute-start | bytes 442376 | tf_op jit(solution)/shard_map/ppermute | solution.py:1684
  (4 other events, 12.4 us)
where the time goes:
time: 233 us; the launch traced here: 231 us
  Pallas kernels  166 us (71%)
  waiting for transfers between devices  28.7 us (12%)
  starting transfers between devices  26.4 us (11%)
  local copies, waits for them, and re-layouts  4.62 us (2%)
  other arithmetic  4.22 us (2%)
    pallas_call x1, Pallas kernels, logits_phase(): pl.pallas_call(logits_kernel, grid=(steps,), in_specs=[rows, rows, pl.Blo...  40.9 us
    pallas_call x2, Pallas kernels, forward(): pl.pallas_call(functools.partial(forward_kernel, train), in_specs=[scalar...  40.4 us
    pallas_call x2, Pallas kernels, gradient_phase(): pl.pallas_call(functools.partial(gradient_kernel, half), grid=(entries //...  33.1 us
    ppermute x16, waiting for transfers between devices, across(): lax.ppermute(value, 'dp', [(i, i ^ mask) for i in range(lax.axis_size('dp...  17.4 us
    ppermute x16, starting transfers between devices, across(): lax.ppermute(value, 'dp', [(i, i ^ mask) for i in range(lax.axis_size('dp...  16.7 us
    ppermute x6, waiting for transfers between devices, swap(): return lax.ppermute(value, 'blk', [(0, 1), (1, 0)])  11.3 us
    pallas_call x1, Pallas kernels, feed_back(): pl.pallas_call(feed_kernel, grid=(1,), in_specs=[scalars()] + [whole_vmem...  11 us
    ppermute x6, starting transfers between devices, swap(): return lax.ppermute(value, 'blk', [(0, 1), (1, 0)])  9.63 us
  transfers between devices with their start and end apart: 22, of which 13 were waited for; matrix products, arithmetic and copies ran while one was open for 2% of the time, Pallas kernels for 24%

commit v1 on v0

--- a/solution.py
+++ b/solution.py
@@ -10,6 +10,7 @@
 HEADS = 12
 HEAD_DIM = 64
 TABLE_SPAN = 2048
+SPLIT_STEPS = 4
 MASKS = (1, 2, 4, 8)
 MASKS_B = (1, 4, 2, 8)
 
@@ -698,6 +699,10 @@
     return [pltpu.with_memory_space_constraint(array, pltpu.HBM) for array in arrays]
 
 
+def near(*arrays):
+    return [pltpu.with_memory_space_constraint(array, pltpu.VMEM) for array in arrays]
+
+
 def scalars():
     return pl.BlockSpec(memory_space=pltpu.SMEM)
 
@@ -835,88 +840,199 @@
     return (norm_s, norm_t, cross / mass_t - norm_t + norm_s)
 
 
-def gradient_kernel(
-    half,
-    diff_ref,
-    expo_ref,
-    table_ref,
-    stats_ref,
-    own_ref,
-    other_ref,
-    total_ref,
-    low_ref,
-    kl_ref,
-    norms,
-):
-    step = pl.program_id(0)
-    count = diff_ref.shape[0]
-    mine = slice(half * count, (half + 1) * count)
-
-    @pl.when(step == 0)
-    def _():
-        norm_s, norm_t, divergence = joined_norms(own_ref[:, mine], other_ref[:, mine])
-        norms[0:1] = norm_s
-        norms[1:2] = norm_t
-        kl_ref[...] = divergence
-        total_ref[...] = jnp.zeros_like(total_ref)
-
-    top_s, mass_s, top_t, mass_t = (stats_ref[0, 8 * i : 8 * i + 8, mine] for i in range(4))
-    first = 0.5 * jnp.exp(top_s - norms[0:1]) * mass_s / mass_t
-    second = first - 0.5 * jnp.exp(top_t - norms[1:2])
-    factors = jnp.concatenate([first, second, jnp.zeros((112, count), jnp.float32)], axis=0).T
+def chunk_factors(stats_ref, norms, rows):
+    top_s, mass_s, top_t, mass_t = (stats_ref[0, 8 * i : 8 * i + 8, rows] for i in range(4))
+    first = 0.5 * jnp.exp(top_s - norms[0:1, rows]) * mass_s / mass_t
+    second = first - 0.5 * jnp.exp(top_t - norms[1:2, rows])
+    pad = jnp.zeros((112, first.shape[1]), jnp.float32)
+    return jnp.concatenate([first, second, pad], axis=0).T
+
+
+def chunk_product(total, diffs, expos, factors, table_ref):
     span = table_ref.shape[0] // 8
-    total = total_ref[...]
     for group in range(2):
         pieces = []
         for part in range(4 * group, 4 * group + 4):
             where = slice(part * span, (part + 1) * span)
             pieces.append(
-                (
-                    diff_ref[:, where].astype(jnp.float32) * factors[:, part : part + 1]
-                    + expo_ref[:, where].astype(jnp.float32) * factors[:, 8 + part : 9 + part]
-                ).astype(jnp.bfloat16)
+                jnp.concatenate(
+                    [
+                        (
+                            diff[:, where].astype(jnp.float32) * factor[:, part : part + 1]
+                            + expo[:, where].astype(jnp.float32) * factor[:, 8 + part : 9 + part]
+                        ).astype(jnp.bfloat16)
+                        for diff, expo, factor in zip(diffs, expos, factors)
+                    ],
+                    axis=0,
+                )
             )
         where = slice(4 * group * span, 4 * (group + 1) * span)
         total = total + dense(jnp.concatenate(pieces, axis=1), table_ref[where, :])
-    total_ref[...] = total
+    return total
+
+
+def gradient_kernel(
+    joint,
+    diff_first,
+    diff_second,
+    expo_first,
+    expo_second,
+    table_ref,
+    stats_ref,
+    own_ref,
+    other_ref,
+    we_hbm,
+    first_out,
+    first_low,
+    second_out,
+    norms_out,
+    we_out,
+    total_ref,
+    load_sem,
+):
+    step = pl.program_id(0)
+    rows = diff_first.shape[0]
+    load = pltpu.make_async_copy(we_hbm, we_out, load_sem)
+    top, bottom = slice(0, rows), slice(rows, 2 * rows)
+
+    @pl.when(step == 0)
+    def _():
+        load.start()
+        norm_s, norm_t, divergence = joined_norms(own_ref[...], other_ref[...])
+        norms_out[0:1] = norm_s
+        norms_out[1:2] = norm_t
+        norms_out[2:3] = divergence
+        total_ref[...] = jnp.zeros_like(total_ref)
+
+    @pl.when(step < joint)
+    def _():
+        total_ref[...] = chunk_product(
+            total_ref[...],
+            (diff_first, diff_second),
+            (expo_first, expo_second),
+            (
+                chunk_factors(stats_ref, norms_out, top),
+                chunk_factors(stats_ref, norms_out, bottom),
+            ),
+            table_ref,
+        )
+
+    @pl.when(step >= joint)
+    def _():
+        total_ref[top] = chunk_product(
+            total_ref[top],
+            (diff_first,),
+            (expo_first,),
+            (chunk_factors(stats_ref, norms_out, top),),
+            table_ref,
+        )
 
     @pl.when(step == pl.num_programs(0) - 1)
     def _():
-        low_ref[...] = total_ref[...].astype(jnp.bfloat16)
-
-
-def gradient_phase(diff, expo, table, stats, own, other, half):
+        first_out[...] = total_ref[top]
+        second_out[...] = total_ref[bottom]
+        first_low[...] = total_ref[top].astype(jnp.bfloat16)
+        load.wait()
+
+
+def gradient_phase(diff, expo, table, stats, own, other, we):
     count, entries = diff.shape
     rows = count // 2
     width = table.shape[1]
     span = TABLE_SPAN
-    wide = pl.BlockSpec((rows, span), lambda j: (half, j))
+    steps = entries // span
+    joint = steps - SPLIT_STEPS
+    top = pl.BlockSpec((rows, span), lambda j: (0, j))
+    bottom = pl.BlockSpec((rows, span), lambda j: (1, jnp.minimum(j, joint - 1)))
     sums = pl.BlockSpec((8, count), lambda j: (0, 0))
     fixed = pl.BlockSpec((rows, width), lambda j: (0, 0))
+    full = jnp.float32
     return pl.pallas_call(
-        functools.partial(gradient_kernel, half),
-        grid=(entries // span,),
+        functools.partial(gradient_kernel, joint),
+        grid=(steps,),
         in_specs=[
-            wide,
-            wide,
+            top,
+            bottom,
+            top,
+            bottom,
             pl.BlockSpec((span, width), lambda j: (j, 0)),
             pl.BlockSpec((1, 40, count), lambda j: (j, 0, 0)),
             sums,
             sums,
+            in_place(),
         ],
-        out_specs=[fixed, fixed, pl.BlockSpec((1, rows), lambda j: (0, 0))],
+        out_specs=[fixed] * 3 + [sums, whole_vmem()],
         out_shape=[
-            jax.ShapeDtypeStruct((rows, width), jnp.float32),
+            jax.ShapeDtypeStruct((rows, width), full),
             jax.ShapeDtypeStruct((rows, width), jnp.bfloat16),
-            jax.ShapeDtypeStruct((1, rows), jnp.float32),
+            jax.ShapeDtypeStruct((rows, width), full),
+            jax.ShapeDtypeStruct((8, count), full),
+            pltpu.VMEM(we.shape, we.dtype),
         ],
-        scratch_shapes=[pltpu.VMEM((8, rows), jnp.float32)],
+        scratch_shapes=[
+            pltpu.VMEM((count, width), full),
+            pltpu.SemaphoreType.DMA,
+        ],
         compiler_params=pltpu.CompilerParams(vmem_limit_bytes=20 << 20),
         cost_estimate=pl.CostEstimate(
             flops=2 * count * width * entries, bytes_accessed=60_000_000, transcendentals=0
         ),
-        name="gradient_second" if half else "gradient_first",
-    )(diff, *far(expo, table), stats, own, other)
+        name="gradient_phase",
+    )(diff, diff, *far(expo, expo, table), stats, own, other, *far(we))
+
+
+def gradient_rest_kernel(
+    diff_ref, expo_ref, table_ref, stats_ref, norms_ref, partial_ref, total_ref, low_ref
+):
+    step = pl.program_id(0)
+    rows = diff_ref.shape[0]
+
+    @pl.when(step == 0)
+    def _():
+        total_ref[...] = partial_ref[...]
+
+    total_ref[...] = chunk_product(
+        total_ref[...],
+        (diff_ref,),
+        (expo_ref,),
+        (chunk_factors(stats_ref, norms_ref, slice(rows, 2 * rows)),),
+        table_ref,
+    )
+
+    @pl.when(step == pl.num_programs(0) - 1)
+    def _():
+        low_ref[...] = total_ref[...].astype(jnp.bfloat16)
+
+
+def gradient_rest(diff, expo, table, stats, norms, partial):
+    count, entries = diff.shape
+    rows, width = partial.shape
+    span = TABLE_SPAN
+    begin = entries // span - SPLIT_STEPS
+    wide = pl.BlockSpec((rows, span), lambda j: (1, begin + j))
+    fixed = pl.BlockSpec((rows, width), lambda j: (0, 0))
+    return pl.pallas_call(
+        gradient_rest_kernel,
+        grid=(SPLIT_STEPS,),
+        in_specs=[
+            wide,
+            wide,
+            pl.BlockSpec((span, width), lambda j: (begin + j, 0)),
+            pl.BlockSpec((1, 40, count), lambda j: (begin + j, 0, 0)),
+            pl.BlockSpec((8, count), lambda j: (0, 0)),
+            fixed,
+        ],
+        out_specs=[fixed, fixed],
+        out_shape=[
+            jax.ShapeDtypeStruct((rows, width), jnp.float32),
+            jax.ShapeDtypeStruct((rows, width), jnp.bfloat16),
+        ],
+        compiler_params=pltpu.CompilerParams(vmem_limit_bytes=18 << 20),
+        cost_estimate=pl.CostEstimate(
+            flops=12_000_000_000, bytes_accessed=1_000_000, transcendentals=0
+        ),
+        name="gradient_rest",
+    )(diff, *far(expo, table), stats, norms, partial)
 
 
 def position(device, masks):
@@ -950,53 +1066,19 @@
     return norm_back(normed, scale, as_row(gain), grad)
 
 
-def feed_loads(wc_hbm, wc, slope_hbm, slope_v, rows, sems):
+def feed_rows(dm, wc, slope, dinner, rows, bias_out, bias_before):
     hidden_width, width = wc.shape
-    loads = []
     for part in range(hidden_width // width):
-        span = pl.ds(part * width, width)
-        loads.append(
-            (
-                pltpu.make_async_copy(wc_hbm.at[span], wc.at[span], sems.at[0, part]),
-                pltpu.make_async_copy(
-                    slope_hbm.at[rows, span], slope_v.at[:, span], sems.at[1, part]
-                ),
-            )
-        )
-    return loads
-
-
-def feed_rows(dm, wc, slope_v, loads, dinner, rows, bias_out, bias_before):
-    width = wc.shape[1]
-    for part, pair in enumerate(loads):
         span = slice(part * width, (part + 1) * width)
-        for load in pair:
-            load.wait()
-        value = nt(dm, wc[span, :]) * slope_v[:, span].astype(jnp.float32)
+        value = nt(dm, wc[span, :]) * slope[rows, span].astype(jnp.float32)
         value = value.astype(jnp.bfloat16)
         dinner[rows, span] = value
         before = 0.0 if bias_before is None else bias_before[:, span]
         bias_out[:, span] = before + row_sums(value)
 
 
-def expand_loads(we_hbm, we, wao_hbm, wao, sems):
-    width = we.shape[0]
-    parts = we.shape[1] // width
-    spans = [pl.ds(part * width, width) for part in range(parts)]
-    return [
-        pltpu.make_async_copy(we_hbm.at[:, span], we.at[:, span], sems.at[part])
-        for part, span in enumerate(spans)
-    ] + [pltpu.make_async_copy(wao_hbm, wao, sems.at[parts])]
-
-
-def branch_rows(dinner, we, loads, after_ref, gain, dy):
-    width = we.shape[0]
-    dh2 = None
-    for part, load in enumerate(loads[:-1]):
-        span = slice(part * width, (part + 1) * width)
-        load.wait()
-        term = nt(dinner[:, span], we[:, span])
-        dh2 = term if dh2 is None else dh2 + term
+def branch_rows(dinner, we, after_ref, gain, dy):
+    dh2 = nt(dinner[...], we[...])
     normed, scale = normalise(after_ref[...])
     dafter = dy + norm_back(normed, scale, as_row(gain), dh2)
     return dafter, row_sums(dh2 * normed), row_sums(dh2)
@@ -1009,10 +1091,10 @@
     after_ref,
     final_gain,
     second_gain,
-    wc_hbm,
-    we_hbm,
-    wao_hbm,
-    slope_hbm,
+    wc,
+    we,
+    wao,
+    slope,
     dm_out,
     dinner_out,
     dafter_out,
@@ -1023,34 +1105,20 @@
     second_gain_out,
     second_shift_out,
     attend_bias_out,
-    wc,
-    we,
-    wao,
-    slope_v,
-    feed_sem,
-    branch_sem,
 ):
     count = own_ref.shape[0]
-    feeding = feed_loads(wc_hbm, wc, slope_hbm, slope_v, pl.ds(0, count), feed_sem)
-    branching = expand_loads(we_hbm, we, wao_hbm, wao, branch_sem)
-    for pair in feeding:
-        for load in pair:
-            load.start()
-    for load in branching:
-        load.start()
     dy = back_to_norm(own_ref, other_ref, y_ref, final_gain)
     dm = dy.astype(jnp.bfloat16)
     dm_out[...] = dm
     contract_bias_out[...] = row_sums(dm)
-    feed_rows(dm, wc, slope_v, feeding, dinner_out, slice(0, count), expand_bias_out, None)
+    feed_rows(dm, wc, slope, dinner_out, slice(0, count), expand_bias_out, None)
     dafter, second_gain_out[...], second_shift_out[...] = branch_rows(
-        dinner_out, we, branching, after_ref, second_gain, dy
+        dinner_out, we, after_ref, second_gain, dy
     )
     dafter_out[...] = dafter
     dbranch = dafter.astype(jnp.bfloat16)
     dbranch_out[...] = dbranch
     attend_bias_out[...] = row_sums(dbranch)
-    branching[-1].wait()
     dmixed_out[...] = nt(dbranch, wao[...]).astype(jnp.bfloat16)
 
 
@@ -1058,7 +1126,6 @@
     rows, width = own.shape
     hidden_width = wc.shape[0]
     low, full = jnp.bfloat16, jnp.float32
-    parts = hidden_width // width
 
     def array(size, kind):
         return jax.ShapeDtypeStruct((rows, size), kind)
@@ -1070,7 +1137,7 @@
     return pl.pallas_call(
         first_kernel,
         grid=(1,),
-        in_specs=[whole_vmem()] * 2 + [top] * 2 + [whole_vmem()] * 2 + [in_place()] * 4,
+        in_specs=[whole_vmem()] * 2 + [top] * 2 + [whole_vmem()] * 6,
         out_specs=[whole_vmem()] * 10,
         out_shape=[
             array(width, low),
@@ -1084,20 +1151,12 @@
             vector(width),
             vector(width),
         ],
-        scratch_shapes=[
-            pltpu.VMEM(wc.shape, low),
-            pltpu.VMEM(we.shape, low),
-            pltpu.VMEM(wao.shape, low),
-            pltpu.VMEM((rows, hidden_width), low),
-            pltpu.SemaphoreType.DMA((2, parts)),
-            pltpu.SemaphoreType.DMA((parts + 1,)),
-        ],
-        compiler_params=pltpu.CompilerParams(vmem_limit_bytes=24 << 20),
+        compiler_params=pltpu.CompilerParams(vmem_limit_bytes=14 << 20),
         cost_estimate=pl.CostEstimate(
             flops=12_000_000_000, bytes_accessed=1_000_000, transcendentals=0
         ),
         name="first_rows",
-    )(own, other, *far(y, after, final_gain, second_gain, wc, we, wao, slope))
+    )(own, other, *far(y, after, final_gain, second_gain), *near(wc, we, wao, slope))
 
 
 def feed_kernel(
@@ -1111,9 +1170,9 @@
     contract_bias_first,
     expand_bias_first,
     wc_hbm,
-    slope_hbm,
-    active_hbm,
-    dinner_hbm,
+    slope,
+    active,
+    dinner_first,
     cw_keep,
     cw_send,
     ew_keep,
@@ -1123,15 +1182,11 @@
     contract_bias_out,
     expand_bias_out,
     wc,
-    slope_v,
-    active_v,
     dinner_v,
     dm_v,
     cw_natural,
     ew_natural,
-    feed_sem,
     load_sem,
-    out_sem,
 ):
     me, blk = place_ref[0], place_ref[1]
     rows = own_ref.shape[0]
@@ -1141,22 +1196,17 @@
     part_width = width // 2
     shards = cw_natural.shape[0]
     chunk = width // shards
-    feeding = feed_loads(wc_hbm, wc, slope_hbm, slope_v, pl.ds(rows, rows), feed_sem)
-    early = pltpu.make_async_copy(dinner_hbm, dinner_v.at[pl.ds(0, rows)], load_sem.at[0])
     loads = [
         pltpu.make_async_copy(
-            active_hbm.at[:, pl.ds(part * width, width)],
-            active_v.at[:, pl.ds(part * width, width)],
-            load_sem.at[1 + part],
+            wc_hbm.at[pl.ds(part * width, width)],
+            wc.at[pl.ds(part * width, width)],
+            load_sem.at[part],
         )
         for part in range(parts)
     ]
     for load in loads:
         load.start()
-    for pair in feeding:
-        for load in pair:
-            load.start()
-    early.start()
+    dinner_v[:rows] = dinner_first[...]
     dy = back_to_norm(own_ref, other_ref, y_ref, final_gain)
     dy_out[...] = dy
     dm = dy.astype(jnp.bfloat16)
@@ -1167,16 +1217,15 @@
     group = shards // parts
     for part in range(parts):
         span = slice(part * width, (part + 1) * width)
-        loads[part].wait()
-        value = tn(active_v[:, span], dm_half).astype(jnp.bfloat16)
+        value = tn(active[:, span], dm_half).astype(jnp.bfloat16)
         cw_natural[part * group : (part + 1) * group] = value.reshape(
             group, width // group, part_width
         )
         place_shards(me, cw_natural, cw_keep, cw_send, MASKS, part * group, group)
-    feed_rows(dm, wc, slope_v, feeding, dinner_v, second, expand_bias_out, expand_bias_first)
-    save = pltpu.make_async_copy(dinner_v.at[pl.ds(rows, rows)], dinner_out, out_sem.at[0])
-    save.start()
-    early.wait()
+    for load in loads:
+        load.wait()
+    feed_rows(dm, wc, slope, dinner_v, second, expand_bias_out, expand_bias_first)
+    dinner_out[...] = dinner_v[second]
     for part in range(parts // 2):
         offset = pl.multiple_of(blk * (hidden_width // 2), width) + part * width
         value = tn(normed_two_ref[...], dinner_v[:, pl.ds(pl.multiple_of(offset, width), width)])
@@ -1188,7 +1237,6 @@
             ].reshape(shards, chunk, part_width)
         rows_at = slice(2 * part * chunk, (2 * part + 2) * chunk)
         place_shards(me, ew_natural, ew_keep, ew_send, MASKS_B, 0, shards, rows_at)
-    save.wait()
 
 
 def feed_back(
@@ -1197,7 +1245,6 @@
     rows, width = own.shape
     count = 2 * rows
     hidden_width = wc.shape[0]
-    parts = hidden_width // width
     low, full = jnp.bfloat16, jnp.float32
     height = hidden_width // shards
     half = jax.ShapeDtypeStruct((shards // 2, height, width // 2), low)
@@ -1209,8 +1256,9 @@
         + [whole_vmem()] * 2
         + [bottom]
         + [whole_vmem()] * 5
-        + [in_place()] * 4,
-        out_specs=[whole_vmem()] * 5 + [in_place(), whole_vmem(), whole_vmem()],
+        + [in_place()]
+        + [whole_vmem()] * 3,
+        out_specs=[whole_vmem()] * 8,
         out_shape=[half] * 4
         + [
             jax.ShapeDtypeStruct((rows, width), full),
@@ -1220,17 +1268,13 @@
         ],
         scratch_shapes=[
             pltpu.VMEM(wc.shape, low),
-            pltpu.VMEM((rows, hidden_width), low),
-            pltpu.VMEM((count, hidden_width), low),
             pltpu.VMEM((count, hidden_width), low),
             pltpu.VMEM((count, width), low),
             pltpu.VMEM((shards, height, width // 2), low),
             pltpu.VMEM((shards, height, width // 2), low),
-            pltpu.SemaphoreType.DMA((2, parts)),
-            pltpu.SemaphoreType.DMA((1 + parts,)),
-            pltpu.SemaphoreType.DMA((1,)),
+            pltpu.SemaphoreType.DMA((hidden_width // width,)),
         ],
-        compiler_params=pltpu.CompilerParams(vmem_limit_bytes=34 << 20),
+        compiler_params=pltpu.CompilerParams(vmem_limit_bytes=26 << 20),
         cost_estimate=pl.CostEstimate(
             flops=12_000_000_000, bytes_accessed=1_000_000, transcendentals=0
         ),
@@ -1243,7 +1287,8 @@
         dm,
         *far(normed_two),
         *biases,
-        *far(wc, slope, active),
+        *far(wc),
+        *near(slope, active),
         dinner,
     )
 
@@ -1259,27 +1304,21 @@
     second_shift_first,
     attend_bias_first,
     dinner_ref,
-    we_hbm,
-    wao_hbm,
+    we,
+    wao,
     dafter_out,
     dmixed_out,
     attend_out,
     second_gain_out,
     second_shift_out,
     attend_bias_out,
-    we,
-    wao,
     dbranch_v,
-    load_sem,
 ):
     blk = place_ref[1]
-    loads = expand_loads(we_hbm, we, wao_hbm, wao, load_sem)
-    for load in loads:
-        load.start()
     rows, width = after_ref.shape
     part_width = width // 2
     dafter, gain_sum, shift_sum = branch_rows(
-        dinner_ref, we, loads, after_ref, second_gain, dy_ref[...]
+        dinner_ref, we, after_ref, second_gain, dy_ref[...]
     )
     dafter_out[...] = dafter
     second_gain_out[...] = second_gain_first[...] + gain_sum
@@ -1288,7 +1327,6 @@
     dbranch_v[:rows] = dbranch_first[...]
     dbranch_v[rows:] = dbranch
     attend_bias_out[...] = attend_bias_first[...] + row_sums(dbranch)
-    loads[-1].wait()
     dmixed_out[...] = nt(dbranch, wao[...]).astype(jnp.bfloat16)
     part = dbranch_v[:, pl.ds(pl.multiple_of(blk * part_width, part_width), part_width)]
     attend_out[...] = tn(mixed_ref[...], part).astype(jnp.bfloat16).reshape(attend_out.shape)
@@ -1296,7 +1334,6 @@
 
 def branch_back(place, dy, after, mixed, second_gain, dbranch, sums, dinner, we, wao, carry, shards):
     rows, width = dy.shape
-    parts = we.shape[1] // width
     low, full = jnp.bfloat16, jnp.float32
     vector = jax.ShapeDtypeStruct((1, width), full)
     bottom = pl.BlockSpec((rows, width), lambda i: (1, 0))
@@ -1304,8 +1341,8 @@
         carrying(branch_kernel, 12, 6, len(carry)),
         grid=(1,),
         in_specs=[scalars(), whole_vmem(), bottom]
-        + [whole_vmem()] * 7
-        + [in_place()] * (2 + len(carry)),
+        + [whole_vmem()] * 9
+        + [in_place()] * len(carry),
         out_specs=[whole_vmem()] * 6 + [in_place()] * len(carry),
         input_output_aliases=aliases(12, 6, carry),
         out_shape=[
@@ -1318,12 +1355,9 @@
         ]
         + shapes_of(carry),
         scratch_shapes=[
-            pltpu.VMEM(we.shape, low),
-            pltpu.VMEM(wao.shape, low),
             pltpu.VMEM((2 * rows, width), low),
-            pltpu.SemaphoreType.DMA((parts + 1,)),
         ],
-        compiler_params=pltpu.CompilerParams(vmem_limit_bytes=22 << 20),
+        compiler_params=pltpu.CompilerParams(vmem_limit_bytes=12 << 20),
         cost_estimate=pl.CostEstimate(
             flops=12_000_000_000, bytes_accessed=1_000_000, transcendentals=0
         ),
@@ -1335,7 +1369,7 @@
         dbranch,
         *sums,
         dinner,
-        *far(we, wao),
+        *near(we, wao),
         *carry,
     )
 
@@ -1641,36 +1675,38 @@
 
 
 def merge_kernel(layout, *refs):
-    total = sum(1 + parts for parts in layout)
-    inputs, outputs = list(refs[:total]), list(refs[total:])
-    done = 0
-    for parts in layout:
-        keep = inputs.pop(0)
+    inputs, outputs = list(refs[: 2 * len(layout)]), list(refs[2 * len(layout) :])
+    for index, mode in enumerate(layout):
+        keep, got = inputs[2 * index], inputs[2 * index + 1]
         half = keep.shape[0] // 2
-        if half == 0:
-            targets = [(outputs[-1].at[done : done + 1], slice(0, 1))]
-            done += 1
+        if mode == "sum":
+            outputs.pop(0)[...] = keep[...] + got[...]
+        elif mode == "pass":
+            outputs.pop(0)[...] = keep[...]
+        elif mode == "halve":
+            outputs.pop(0)[...] = keep[:half] + got[:half]
+            outputs.pop(0)[...] = keep[half:] + got[half:]
         else:
-            targets = [(outputs.pop(0), slice(0, half)), (outputs.pop(0), slice(half, 2 * half))]
-        row = 0
-        for _ in range(parts):
-            got = inputs.pop(0)
-            rows = slice(row, row + got.shape[1])
-            row = rows.stop
-            for target, which in targets:
-                target[:, rows] = keep[which, rows] + got[which]
-
-
-def merge(*pairs):
-    shapes, finals = [], [pair[0] for pair in pairs if pair[0].shape[0] == 1]
-    for keep, *_ in pairs:
-        if keep.shape[0] > 1:
-            shapes += [jax.ShapeDtypeStruct((keep.shape[0] // 2, *keep.shape[1:]), keep.dtype)] * 2
-    if finals:
-        shapes.append(jax.ShapeDtypeStruct((len(finals), *finals[0].shape[1:]), finals[0].dtype))
-    arrays = [array for pair in pairs for array in pair]
+            place = layout[:index].count("stack")
+            if place == 0:
+                stacked = (outputs.pop(0), outputs.pop(0))
+            stacked[0][place : place + half] = keep[:half] + got[:half]
+            stacked[1][place : place + half] = keep[half:] + got[half:]
+
+
+def merge(*groups):
+    layout = [mode for mode, _, _ in groups]
+    shapes = []
+    for index, (mode, keep, _) in enumerate(groups):
+        size = keep.shape[0]
+        if mode in ("sum", "pass"):
+            shapes.append(jax.ShapeDtypeStruct(keep.shape, keep.dtype))
+        elif mode == "halve" or "stack" not in layout[:index]:
+            rows = size // 2 * (layout.count("stack") if mode == "stack" else 1)
+            shapes += [jax.ShapeDtypeStruct((rows, *keep.shape[1:]), keep.dtype)] * 2
+    arrays = [array for _, keep, got in groups for array in (keep, got)]
     return pl.pallas_call(
-        functools.partial(merge_kernel, [len(pair) - 1 for pair in pairs]),
+        functools.partial(merge_kernel, layout),
         in_specs=[whole_vmem()] * len(arrays),
         out_specs=[whole_vmem()] * len(shapes),
         out_shape=shapes,
@@ -1678,6 +1714,74 @@
         cost_estimate=pl.CostEstimate(flops=1_000_000, bytes_accessed=1_000_000, transcendentals=0),
         name="merge",
     )(*arrays)
+
+
+def feed_finish_kernel(place_ref, own_ref, other_ref, contract_out, expand_out):
+    blk = place_ref[1]
+    part = own_ref.shape[2]
+    chunk = expand_out.shape[0]
+    half = expand_out.shape[1] // 2
+    for side, ref in ((blk, own_ref), (1 - blk, other_ref)):
+        contract_out[:, pl.ds(pl.multiple_of(side * part, part), part)] = ref[0].astype(jnp.float32)
+        for index in range(half // part):
+            offset = side * half + index * part
+            expand_out[:, pl.ds(pl.multiple_of(offset, part), part)] = ref[
+                1, index * chunk : (index + 1) * chunk
+            ].astype(jnp.float32)
+
+
+def feed_finish(place, own, other, chunk):
+    _, rows, part = own.shape
+    full = jnp.float32
+    return pl.pallas_call(
+        feed_finish_kernel,
+        in_specs=[scalars()] + [whole_vmem()] * 2,
+        out_specs=[whole_vmem()] * 2,
+        out_shape=[
+            jax.ShapeDtypeStruct((rows, 2 * part), full),
+            jax.ShapeDtypeStruct((chunk, 2 * part * rows // chunk), full),
+        ],
+        compiler_params=pltpu.CompilerParams(vmem_limit_bytes=16 << 20),
+        cost_estimate=pl.CostEstimate(flops=1_000_000, bytes_accessed=1_000_000, transcendentals=0),
+        name="feed_finish",
+    )(place, own, other)
+
+
+def finish_kernel(
+    place_ref, own_ref, other_ref, keep_ref, got_ref, _, attend_out, project_out, *vector_outs
+):
+    blk = place_ref[1]
+    chunk, width = attend_out.shape
+    part = width // 2
+    for side, ref in ((blk, own_ref), (1 - blk, other_ref)):
+        for index in range(4):
+            value = ref[index * chunk : (index + 1) * chunk].astype(jnp.float32)
+            if index == 0:
+                target, offset = attend_out, side * part
+            else:
+                target, offset = project_out, (index - 1) * width + side * part
+            target[:, pl.ds(pl.multiple_of(offset, part), part)] = value
+    total = keep_ref[0] + got_ref[0]
+    for index, out in enumerate(vector_outs):
+        out[...] = total[index : index + 1, : out.shape[1]]
+
+
+def finish(place, own, other, keep, got, ready, chunk, sizes):
+    width = 2 * own.shape[1]
+    full = jnp.float32
+    return pl.pallas_call(
+        finish_kernel,
+        in_specs=[scalars()] + [whole_vmem()] * 4 + [in_place()],
+        out_specs=[whole_vmem()] * (2 + len(sizes)),
+        out_shape=[
+            jax.ShapeDtypeStruct((chunk, width), full),
+            jax.ShapeDtypeStruct((chunk, 3 * width), full),
+        ]
+        + [jax.ShapeDtypeStruct((1, size), full) for size in sizes],
+        compiler_params=pltpu.CompilerParams(vmem_limit_bytes=16 << 20),
+        cost_estimate=pl.CostEstimate(flops=1_000_000, bytes_accessed=1_000_000, transcendentals=0),
+        name="finish",
+    )(place, own, other, keep, got, ready)
 
 
 def swap(value):
@@ -1718,11 +1822,11 @@
     diff, expo, stats, sums = logits_phase(rows_s, rows_t, table)
     gain, shift, wpi, qvb, wao, bao, gain_two, shift_two, we, be, wc, bc = student
     sums_other = swap(sums)
-    own_first, low_first, kl_first = gradient_phase(diff, expo, table, stats, sums, sums_other, 0)
+    own_first, low_first, partial, norms, we = gradient_phase(
+        diff, expo, table, stats, sums, sums_other, we
+    )
     got_first = swap(low_first)
-    own_second, low_second, kl_second = gradient_phase(
-        diff, expo, table, stats, sums, sums_other, 1
-    )
+    own_second, low_second = gradient_rest(diff, expo, table, stats, norms, partial)
     got_second = swap(low_second)
     dm, dinner, dafter_first, dbranch, dmixed_first, dbc, dbe, *branch_sums = first_rows(
         own_first, got_first, y, after, final_gain, gain_two, wc, we, wao, slope
@@ -1769,19 +1873,18 @@
         place, joined, probs, dmixed, normed, attend, (cw_keep, ew_keep), rows, shards
     )
     got = across(send, MASKS[0])
-    cw_keep, cw_send, ew_keep, ew_send = merge((cw_keep, cw_got), (ew_keep, ew_got))
+    cw_keep, cw_send, ew_keep, ew_send = merge(("halve", cw_keep, cw_got), ("halve", ew_keep, ew_got))
     cw_got = across(cw_send, MASKS[2])
     ew_got = across(ew_send, MASKS_B[2])
     *other_grads, keep, cw_keep, ew_keep = attend_back(
         place, joined, probs, dmixed, (keep, cw_keep, ew_keep), rows
     )
-    keep, send, cw_keep, cw_send, ew_keep, ew_send = merge(
-        (keep, got), (cw_keep, cw_got), (ew_keep, ew_got)
+    keep, send, both_keep, both_send = merge(
+        ("halve", keep, got), ("stack", cw_keep, cw_got), ("stack", ew_keep, ew_got)
     )
     got = across(send, MASKS[1])
-    cw_got = across(cw_send, MASKS[3])
-    ew_got = across(ew_send, MASKS_B[3])
-    input_grad, vector_keep, vector_send, keep, cw_keep, ew_keep = input_back(
+    both_got = across(both_send, MASKS[3])
+    input_grad, vector_keep, vector_send, keep, both_keep = input_back(
         place,
         hidden,
         other,
@@ -1790,41 +1893,43 @@
         gain,
         (dbao, dgain_two, dshift_two, dbe, dbc),
         wpi,
-        (keep, cw_keep, ew_keep),
+        (keep, both_keep),
         shards,
     )
     vector_got = across(vector_send, MASKS[0])
-    keep, send, vector_keep, vector_send, both = merge(
-        (keep, got), (cw_keep, cw_got), (ew_keep, ew_got), (vector_keep, vector_got)
-    )
-    got, both_other = across(send, MASKS[2]), swap(both)
-    vector_got = across(vector_send, MASKS[1])
-    keep, send, vector_keep, vector_send = merge((keep, got), (vector_keep, vector_got))
-    got, vector_got = across(send, MASKS[3]), across(vector_send, MASKS[2])
-    vector_keep, vector_send, last = merge((keep, got), (vector_keep, vector_got))
+    keep, send, both, vector_keep, vector_send = merge(
+        ("halve", keep, got),
+        ("sum", both_keep, both_got),
+        ("halve", vector_keep, vector_got),
+    )
+    got, vector_got = across(send, MASKS[2]), across(vector_send, MASKS[1])
+    keep, send, both, vector_keep, vector_send = merge(
+        ("halve", keep, got),
+        ("pass", both, both),
+        ("halve", vector_keep, vector_got),
+    )
+    got, vector_got, both_other = (
+        across(send, MASKS[3]),
+        across(vector_send, MASKS[2]),
+        swap(both),
+    )
+    last, vector_keep, vector_send = merge(
+        ("sum", keep, got), ("halve", vector_keep, vector_got)
+    )
     last = last[0]
     last_other = swap(last)
-    vectors = (vector_keep + across(vector_send, MASKS[3]))[0]
-    cw, ew, cw_other, ew_other = both[0], both[1], both_other[0], both_other[1]
+    vector_got = across(vector_send, MASKS[3])
     chunk = width // shards
-
-    def wide(own, other):
-        own, other = (part.reshape(-1, chunk, part.shape[1]) for part in (own, other))
-        order = [own[i] for i in range(own.shape[0])], [other[i] for i in range(own.shape[0])]
-        return order
-
-    grad_cw = both_halves(cw, cw_other, blk)
-    own, other = wide(ew, ew_other)
-    grad_ew = both_halves(jnp.concatenate(own, axis=1), jnp.concatenate(other, axis=1), blk)
-    own, other = wide(last, last_other)
-    grad_ao = both_halves(own[0], other[0], blk)
-    grad_pi = jnp.concatenate([both_halves(own[i], other[i], blk) for i in (1, 2, 3)], axis=1)
+    grad_cw, grad_ew = feed_finish(place, both, both_other, chunk)
     sizes = (chunk, chunk, 2 * chunk, chunk, chunk, chunk, be.shape[0] // shards, chunk)
+    grad_ao, grad_pi, *vectors = finish(
+        place, last, last_other, vector_keep, vector_got, grad_cw, chunk, sizes
+    )
     dgain, dshift, dqvb, dbao, dgain_two, dshift_two, dbe, dbc = (
-        vectors[index, :size] for index, size in enumerate(sizes)
+        vector.reshape(-1) for vector in vectors
     )
     return (
-        jnp.where(blk == 0, kl_first[0], kl_second[0]),
+        lax.dynamic_slice_in_dim(norms[2], blk * rows, rows),
         input_grad,
         dgain,
         dshift,

time: 233 us -> 224 us (0.961)
  Pallas kernels: 166 us -> 157 us
  other arithmetic: 4.22 us -> 0.34 us
  waiting for transfers between devices: 28.7 us -> 32.3 us
  starting transfers between devices: 26.4 us -> 23.9 us
    pallas_call x1, Pallas kernels: 9.56 us -> 5.8 us  [first_rows(): pl.pallas_call(first_kernel, grid=(1,), in_specs=[whole_vmem()] * 2 + [to...]
    ppermute x16 -> x15, waiting for transfers between devices: 17.4 us -> 21 us  [across(): lax.ppermute(value, 'dp', [(i, i ^ mask) for i in range(lax.axis_size('dp...]
    unnamed x22 -> x28, local copies, waits for them, and re-layouts: 2.91 us -> 6.21 us
    ppermute x16 -> x15, starting transfers between devices: 16.7 us -> 14.3 us  [across(): lax.ppermute(value, 'dp', [(i, i ^ mask) for i in range(lax.axis_size('dp...]
    pallas_call x7 -> x9, Pallas kernels: 33.8 us -> 33.3 us  [the longest x1 20.2 us: gradient_phase(): pl.pallas_call(functools.partial(gradient_kernel, joint), grid=(steps,),...]
  transfers between devices with their start and end apart: 22 -> 21, of which waited for: 13 -> 13; matrix products, arithmetic and copies ran while one was open for 2% -> 0% of each run, Pallas kernels for 24% -> 20%
where the time goes in v1:
time: 224 us; the launch traced here: 222 us
  Pallas kernels  157 us (70%)
  waiting for transfers between devices  32.3 us (14%)
  starting transfers between devices  23.9 us (11%)
  local copies, waits for them, and re-layouts  6.78 us (3%)
    pallas_call x2, Pallas kernels, forward(): pl.pallas_call(functools.partial(forward_kernel, train), in_specs=[scalar...  40.5 us
    pallas_call x1, Pallas kernels, logits_phase(): pl.pallas_call(logits_kernel, grid=(steps,), in_specs=[rows, rows, pl.Blo...  39.3 us
    ppermute x15, waiting for transfers between devices, across(): lax.ppermute(value, 'dp', [(i, i ^ mask) for i in range(lax.axis_size('dp...  21 us
    pallas_call x1, Pallas kernels, gradient_phase(): pl.pallas_call(functools.partial(gradient_kernel, joint), grid=(steps,),...  20.2 us
    ppermute x15, starting transfers between devices, across(): lax.ppermute(value, 'dp', [(i, i ^ mask) for i in range(lax.axis_size('dp...  14.3 us
    ppermute x6, waiting for transfers between devices, swap(): return lax.ppermute(value, 'blk', [(0, 1), (1, 0)])  11.3 us
    pallas_call x1, Pallas kernels, feed_back(): pl.pallas_call(feed_kernel, grid=(1,), in_specs=[scalars()] + [whole_vmem...  10.3 us
    ppermute x6, starting transfers between devices, swap(): return lax.ppermute(value, 'blk', [(0, 1), (1, 0)])  9.53 us
  transfers between devices with their start and end apart: 21, of which 13 were waited for; matrix products, arithmetic and copies ran while one was open for 0% of the time, Pallas kernels for 20%

profile of v1, /device:TPU:0, one launch (start us, length us, event | category | flops | bytes accessed | tf_op | source)
XLA Modules:
  0.0 221.6 jit_solution(11525050403299726717)
XLA Ops:
  0.6 3.0 %collective-permute-start = (bf16[256,768]{1,0:T(8,128)(2,1)}, bf16[256,768]{1,0:T(8,128)(2,1)S(1)}, u32[]{:S(2)}, u32[]{:S(2)}) collective-permute-start(bf16[256,768]{1,0:T(8,128)(2,1)} %refs_1_.5), channel_id=1, source_target_pairs={{0,1},{1,0},{2,3},{3,2},{4,5},{5,4},{6,7},{7,6},{8,9},{9,8},{10,11... | collective-permute-start | bytes 1179656 | tf_op jit(solution)/shard_map/ppermute | solution.py:1788
  3.8 9.2 %collective-permute-done.refs_3_.refs_2_ = bf16[256,768]{1,0:T(8,128)(2,1)S(1)} collective-permute-done((bf16[256,768]{1,0:T(8,128)(2,1)}, bf16[256,768]{1,0:T(8,128)(2,1)S(1)}, u32[]{:S(2)}, u32[]{:S(2)}) %collective-permute-start) | collective-permute-done | bytes 393248 | tf_op jit(solution)/shard_map/ppermute | solution.py:1788
  14.7 18.2 %forward_teacher.1.teacher_ref = bf16[512,768]{1,0:T(8,128)(2,1)S(1)} custom-call(s32[2]{0:T(128)S(1)} %pad_add_fusion.refs_0_.place_ref, s32[1,4]{1,0:T(1,128)S(1)} %copy-done.9, bf16[256,768]{1,0:T(8,128)(2,1)S(1)} %copy-done.7, bf16[256,768]{1,0:T(8,128)(2,1)S(1)} %collective-permute-done.refs_3_.refs_2_, f32[768]{0:T(1024)} %refs_4_.4, f32[768]{0:T(1024)} %refs_5_.3, ...), custom_call_target="tpu_custom_call" | custom-call | flops 8000000000 | bytes 20000000 | tf_op jit(solution)/shard_map/forward_teacher/pallas_call | solution.py:734
  32.9 22.3 %forward_student.1 = (bf16[512,768]{1,0:T(8,128)(2,1)}, bf16[512,768]{1,0:T(8,128)(2,1)}, bf16[512,2304]{1,0:T(8,128)(2,1)}, bf16[12,512,512]{2,1,0:T(8,128)(2,1...) custom-call(s32[2]{0:T(128)} %copy-done.1, ...), custom_call_target="tpu_custom_call" | custom-call | flops 8000000000 | bytes 20000000 | tf_op jit(solution)/shard_map/forward_student/pallas_call | solution.py:734
  56.3 39.3 %logits_phase.1 = (bf16[512,16384]{1,0:T(8,128)(2,1)S(1)}, bf16[512,16384]{1,0:T(8,128)(2,1)}, f32[8,40,512]{2,1,0:T(8,128)S(1)}, f32[8,512]{1,0:T(8,128)S(1)}) custom-call(bf16[512,768]{1,0:T(8,128)(2,1)S(1)} %copy-done.13, bf16[512,768]{1,0:T(8,128)(2,1)S(1)} %forward_teacher.1.teacher_ref, bf16[16384,768]{1,0:T(8,128)(2,1)} %table_ref.5), custom_call_target="tpu_custom_call" | custom-call | flops 25769803776 | bytes 60000000 | tf_op jit(solution)/shard_map/logits_phase/pallas_call | solution.py:807
  95.6 1.7 collective-permute-start.1
  97.3 2.0 collective-permute-done.1.other_ref
  99.3 20.2 %gradient_phase.1 = (f32[256,768]{1,0:T(8,128)S(1)}, bf16[256,768]{1,0:T(8,128)(2,1)S(1)}, f32[256,768]{1,0:T(8,128)S(1)}, f32[8,512]{1,0:T(8,128)S(1)}, bf16[768,3072]{1,0:T(8,128)(2,1)S(1)}) custom-call(bf16[512,16384]{1,0:T(8,128)(2,1)S(1)} %get-tuple-element.113.diff_first.diff_second.diff_ref, ...), custom_call_target="tpu_custom_call" | custom-call | flops 12884901888 | bytes 60000000 | tf_op jit(solution)/shard_map/gradient_phase/pallas_call | solution.py:950
  119.6 1.8 collective-permute-start.2
  121.4 9.3 %gradient_rest.1 = (f32[256,768]{1,0:T(8,128)S(1)}, bf16[256,768]{1,0:T(8,128)(2,1)S(1)}) custom-call(bf16[512,16384]{1,0:T(8,128)(2,1)S(1)} %get-tuple-element.113.diff_first.diff_second.diff_ref, bf16[512,16384]{1,0:T(8,128)(2,1)} %get-tuple-element.114.expo_first.expo_second.expo_ref, bf16[16384,768]{1,0:T(8,128)(2,1)} %table_ref.5, ...), custom_call_target="tpu_custom_call" | custom-call | flops 12000000000 | bytes 1000000 | tf_op jit(solution)/shard_map/gradient_rest/pallas_call | solution.py:1014
  132.4 2.3 %copy-done.3 = bf16[3072,768]{1,0:T(8,128)(2,1)S(1)} copy-done((bf16[3072,768]{1,0:T(8,128)(2,1)S(1)}, bf16[3072,768]{1,0:T(8,128)(2,1)}, u32[]{:S(2)}) %copy-start.3) | copy-done | bytes 4718616
  134.7 5.8 %first_rows.1 = (bf16[256,768]{1,0:T(8,128)(2,1)S(1)}, bf16[256,3072]{1,0:T(8,128)(2,1)S(1)}, f32[256,768]{1,0:T(8,128)S(1)}, bf16[256,768]{1,0:T(8,128)(2,1)S(1...) custom-call(f32[256,768]{1,0:T(8,128)S(1)} %get-tuple-element.120.ow, ...), custom_call_target="tpu_custom_call" | custom-call | flops 12000000000 | bytes 1000000 | tf_op jit(solution)/shard_map/first_rows/pallas_call | solution.py:1137
  140.6 10.3 %feed_back.1 = (bf16[8,192,384]{2,1,0:T(8,128)(2,1)S(1)}, bf16[8,192,384]{2,1,0:T(8,128)(2,1)S(1)}, bf16[8,192,384]{2,1,0:T(8,128)(2,1)S(1)}, bf16[8,192,384]{2,...) custom-call(s32[2]{0:T(128)S(1)} %copy-done.2, ...), custom_call_target="tpu_custom_call" | custom-call | flops 12000000000 | bytes 1000000 | tf_op jit(solution)/shard_map/feed_back/pallas_call | solution.py:1252
  151.4 4.9 %branch_back.1 = (f32[256,768]{1,0:T(8,128)S(1)}, bf16[256,768]{1,0:T(8,128)(2,1)S(1)}, bf16[16,48,384]{2,1,0:T(8,128)(2,1)S(1)}, f32[1,768]{1,0:T(1,128)S(1)}, ...) custom-call(s32[2]{0:T(128)S(1)} %copy-done.2, ...), custom_call_target="tpu_custom_call", output_to_operand_aliasing={{6}: (12, {}), {7}: (13, {})} | custom-call | flops 12000000000 | bytes 1000000 | tf_op jit(solution)/shard_map/branch_back/pallas_call | solution.py:1340
  159.8 8.5 %project_back.1 = (bf16[512,384]{1,0:T(8,128)(2,1)S(1)}, bf16[512,384]{1,0:T(8,128)(2,1)S(1)}, bf16[512,384]{1,0:T(8,128)(2,1)S(1)}, bf16[8,192,384]{2,1,0:T(8,1...) custom-call(s32[2]{0:T(128)S(1)} %copy-done.2, ...), custom_call_target="tpu_custom_call", output_to_operand_aliasing={{5}: (9, {}), {6}: (10, {})} | custom-call | flops 12000000000 | bytes 1000000 | tf_op jit(solution)/shard_map/project_back/pallas_call | solution.py:1540
  168.5 3.4 %collective-permute-done.6.refs_1_ = bf16[4,192,384]{2,1,0:T(8,128)(2,1)S(1)} collective-permute-done((bf16[4,192,384]{2,1,0:T(8,128)(2,1)S(1)}, bf16[4,192,384]{2,1,0:T(8,128)(2,1)S(1)}, u32[]{:S(2)}, u32[]{:S(2)}) %collective-permute-start.6) | collective-permute-done | bytes 589856 | tf_op jit(solution)/shard_map/ppermute | solution.py:1669
  175.7 6.3 %attend_back.1 = (bf16[512,384]{1,0:T(8,128)(2,1)S(1)}, bf16[512,384]{1,0:T(8,128)(2,1)S(1)}, bf16[512,384]{1,0:T(8,128)(2,1)S(1)}, bf16[8,192,384]{2,1,0:T(8,12...) custom-call(s32[2]{0:T(128)S(1)} %copy-done.2, ...), custom_call_target="tpu_custom_call", output_to_operand_aliasing={{3}: (7, {}), {4}: (8, {}), {5}: (9, {})} | custom-call | flops 12000000000 | bytes 1000000 | tf_op jit(solution)/shard_map/attend_back/pallas_call | solution.py:1511
  183.0 2.6 %collective-permute-start.12 = (bf16[2,192,384]{2,1,0:T(8,128)(2,1)S(1)}, bf16[2,192,384]{2,1,0:T(8,128)(2,1)S(1)}, u32[]{:S(2)}, u32[]{:S(2)}) collective-permute-start(bf16[2,192,384]{2,1,0:T(8,128)(2,1)S(1)} %get-tuple-element.182), channel_id=1, source_target_pairs={{0,16},{2,18},{4,20},{6,22},{8,24},{10,26},{12,28},{14,30},{16,0},... | collective-permute-start | bytes 884744 | tf_op jit(solution)/shard_map/ppermute | solution.py:1669
  186.4 8.2 %input_back.1 = (f32[256,768]{1,0:T(8,128)}, f32[8,8,256]{2,1,0:T(8,128)S(1)}, f32[8,8,256]{2,1,0:T(8,128)S(1)}, bf16[4,192,384]{2,1,0:T(8,128)(2,1)S(1)}, bf16[2,192,384]{2,1,0:T(8,128)(2,1)S(1)}) custom-call(s32[2]{0:T(128)S(1)} %copy-done.2, bf16[256,768]{1,0:T(8,128)(2,1)} %refs_1_.5, ...), custom_call_target="tpu_custom_call", output_to_operand_aliasing={{3}: (18, {}), {4}: (19, {})} | custom-call | flops 12000000000 | bytes 1000000 | tf_op jit(solution)/shard_map/input_back/pallas_call | solution.py:1645
  200.4 2.6 %collective-permute-done.15.refs_5_ = f32[4,8,256]{2,1,0:T(8,128)S(1)} collective-permute-done((f32[4,8,256]{2,1,0:T(8,128)S(1)}, f32[4,8,256]{2,1,0:T(8,128)S(1)}, u32[]{:S(2)}, u32[]{:S(2)}) %collective-permute-start.15) | collective-permute-done | bytes 32800 | tf_op jit(solution)/shard_map/ppermute | solution.py:1669
  203.0 3.1 %collective-permute-done.14.refs_1_ = bf16[2,192,384]{2,1,0:T(8,128)(2,1)S(1)} collective-permute-done((bf16[2,192,384]{2,1,0:T(8,128)(2,1)S(1)}, bf16[2,192,384]{2,1,0:T(8,128)(2,1)S(1)}, u32[]{:S(2)}, u32[]{:S(2)}) %collective-permute-start.14) | collective-permute-done | bytes 294944 | tf_op jit(solution)/shard_map/ppermute | solution.py:1669
  207.3 1.7 collective-permute-start.17
  209.0 2.0 collective-permute-done.17.refs_3_
  211.0 2.5 %collective-permute-done.16.refs_1_ = bf16[1,192,384]{2,1,0:T(8,128)(2,1)S(1)} collective-permute-done((bf16[1,192,384]{2,1,0:T(8,128)(2,1)S(1)}, bf16[1,192,384]{2,1,0:T(8,128)(2,1)S(1)}, u32[]{:S(2)}, u32[]{:S(2)}) %collective-permute-start.16) | collective-permute-done | bytes 147488 | tf_op jit(solution)/shard_map/ppermute | solution.py:1669
  (69 shorter events, 28.8 us)
Async XLA Ops:
  0.6 12.4 %collective-permute-start = (bf16[256,768]{1,0:T(8,128)(2,1)}, bf16[256,768]{1,0:T(8,128)(2,1)S(1)}, u32[]{:S(2)}, u32[]{:S(2)}) collective-permute-start(bf16[256,768]{1,0:T(8,128)(2,1)} %refs_1_.5), channel_id=1, source_target_pairs={{0,1},{1,0},{2,3},{3,2},{4,5},{5,4},{6,7},{7,6},{8,9},{9,8},{10,11... | collective-permute-start | bytes 1179656 | tf_op jit(solution)/shard_map/ppermute | solution.py:1788
  3.8 29.1 %copy-start.1 = (s32[2]{0:T(128)}, s32[2]{0:T(128)S(1)}, u32[]{:S(2)}) copy-start(s32[2]{0:T(128)S(1)} %pad_add_fusion.refs_0_.place_ref) | copy-start | bytes 28
  14.7 18.2 %copy-start.8 = (bf16[256,768]{1,0:T(8,128)(2,1)}, bf16[256,768]{1,0:T(8,128)(2,1)S(1)}, u32[]{:S(2)}) copy-start(bf16[256,768]{1,0:T(8,128)(2,1)S(1)} %collective-permute-done.refs_3_.refs_2_) | copy-start | bytes 1179652
  95.6 3.7 %collective-permute-start.1 = (f32[8,512]{1,0:T(8,128)S(1)}, f32[8,512]{1,0:T(8,128)S(1)}, u32[]{:S(2)}, u32[]{:S(2)}) collective-permute-start(f32[8,512]{1,0:T(8,128)S(1)} %get-tuple-element.116.own_ref), channel_id=1, source_target_pairs={{0,1},{1,0},{2,3},{3,2},{4,5},{5,4},{6,7},{7,6},{8,9},{9,8},{10,11... | collective-permute-start | bytes 49160 | tf_op jit(solution)/shard_map/ppermute | solution.py:1788
  119.6 12.8 %copy-start.4 = (bf16[768,3072]{1,0:T(8,128)(2,1)}, bf16[768,3072]{1,0:T(8,128)(2,1)S(1)}, u32[]{:S(2)}) copy-start(bf16[768,3072]{1,0:T(8,128)(2,1)S(1)} %get-tuple-element.124.we.refs_10_) | copy-start | bytes 14155780
  119.6 12.7 %collective-permute-start.2 = (bf16[256,768]{1,0:T(8,128)(2,1)S(1)}, bf16[256,768]{1,0:T(8,128)(2,1)S(1)}, u32[]{:S(2)}, u32[]{:S(2)}) collective-permute-start(bf16[256,768]{1,0:T(8,128)(2,1)S(1)} %get-tuple-element.121), channel_id=1, source_target_pairs={{0,1},{1,0},{2,3},{3,2},{4,5},{5,4},{6,7},{7,6},{8,9},{9,8},{10,11... | collective-permute-start | bytes 1179656 | tf_op jit(solution)/shard_map/ppermute | solution.py:1788
  130.8 9.8 %collective-permute-start.3 = (bf16[256,768]{1,0:T(8,128)(2,1)S(1)}, bf16[256,768]{1,0:T(8,128)(2,1)S(1)}, u32[]{:S(2)}, u32[]{:S(2)}) collective-permute-start(bf16[256,768]{1,0:T(8,128)(2,1)S(1)} %get-tuple-element.129), channel_id=1, source_target_pairs={{0,1},{1,0},{2,3},{3,2},{4,5},{5,4},{6,7},{7,6},{8,9},{9,8},{10,11... | collective-permute-start | bytes 1179656 | tf_op jit(solution)/shard_map/ppermute | solution.py:1788
  150.9 5.5 %collective-permute-start.4 = (bf16[8,192,384]{2,1,0:T(8,128)(2,1)S(1)}, bf16[8,192,384]{2,1,0:T(8,128)(2,1)S(1)}, u32[]{:S(2)}, u32[]{:S(2)}) collective-permute-start(bf16[8,192,384]{2,1,0:T(8,128)(2,1)S(1)} %get-tuple-element.149), channel_id=1, source_target_pairs={{0,2},{2,0},{4,6},{6,4},{8,10},{10,8},{12,14},{14,12},{16,18},{18,... | collective-permute-start | bytes 3538952 | tf_op jit(solution)/shard_map/ppermute | solution.py:1669
  150.9 7.1 %collective-permute-start.5 = (bf16[8,192,384]{2,1,0:T(8,128)(2,1)S(1)}, bf16[8,192,384]{2,1,0:T(8,128)(2,1)S(1)}, u32[]{:S(2)}, u32[]{:S(2)}) collective-permute-start(bf16[8,192,384]{2,1,0:T(8,128)(2,1)S(1)} %get-tuple-element.151), channel_id=1, source_target_pairs={{0,2},{2,0},{4,6},{6,4},{8,10},{10,8},{12,14},{14,12},{16,18},{18,... | collective-permute-start | bytes 3538952 | tf_op jit(solution)/shard_map/ppermute | solution.py:1669
  156.5 15.4 %collective-permute-start.6 = (bf16[4,192,384]{2,1,0:T(8,128)(2,1)S(1)}, bf16[4,192,384]{2,1,0:T(8,128)(2,1)S(1)}, u32[]{:S(2)}, u32[]{:S(2)}) collective-permute-start(bf16[4,192,384]{2,1,0:T(8,128)(2,1)S(1)} %get-tuple-element.212), channel_id=1, source_target_pairs={{0,4},{2,6},{4,0},{6,2},{8,12},{10,14},{12,8},{14,10},{16,20},{18,... | collective-permute-start | bytes 1769480 | tf_op jit(solution)/shard_map/ppermute | solution.py:1669
  158.2 15.1 %collective-permute-start.7 = (bf16[4,192,384]{2,1,0:T(8,128)(2,1)S(1)}, bf16[4,192,384]{2,1,0:T(8,128)(2,1)S(1)}, u32[]{:S(2)}, u32[]{:S(2)}) collective-permute-start(bf16[4,192,384]{2,1,0:T(8,128)(2,1)S(1)} %get-tuple-element.210), channel_id=1, source_target_pairs={{0,8},{2,10},{4,12},{6,14},{8,0},{10,2},{12,4},{14,6},{16,24},{18,... | collective-permute-start | bytes 1769480 | tf_op jit(solution)/shard_map/ppermute | solution.py:1669
  168.4 14.3 %collective-permute-start.8 = (bf16[8,192,384]{2,1,0:T(8,128)(2,1)S(1)}, bf16[8,192,384]{2,1,0:T(8,128)(2,1)S(1)}, u32[]{:S(2)}, u32[]{:S(2)}) collective-permute-start(bf16[8,192,384]{2,1,0:T(8,128)(2,1)S(1)} %get-tuple-element.171), channel_id=1, source_target_pairs={{0,2},{2,0},{4,6},{6,4},{8,10},{10,8},{12,14},{14,12},{16,18},{18,... | collective-permute-start | bytes 3538952 | tf_op jit(solution)/shard_map/ppermute | solution.py:1669
  173.5 8.5 %collective-permute-start.9 = (bf16[2,192,384]{2,1,0:T(8,128)(2,1)S(1)}, bf16[2,192,384]{2,1,0:T(8,128)(2,1)S(1)}, u32[]{:S(2)}, u32[]{:S(2)}) collective-permute-start(bf16[2,192,384]{2,1,0:T(8,128)(2,1)S(1)} %get-tuple-element.173), channel_id=1, source_target_pairs={{0,8},{2,10},{4,12},{6,14},{8,0},{10,2},{12,4},{14,6},{16,24},{18,... | collective-permute-start | bytes 884744 | tf_op jit(solution)/shard_map/ppermute | solution.py:1669
  175.1 7.6 %collective-permute-start.10 = (bf16[2,192,384]{2,1,0:T(8,128)(2,1)S(1)}, bf16[2,192,384]{2,1,0:T(8,128)(2,1)S(1)}, u32[]{:S(2)}, u32[]{:S(2)}) collective-permute-start(bf16[2,192,384]{2,1,0:T(8,128)(2,1)S(1)} %get-tuple-element.175), channel_id=1, source_target_pairs={{0,4},{2,6},{4,0},{6,2},{8,12},{10,14},{12,8},{14,10},{16,20},{18,... | collective-permute-start | bytes 884744 | tf_op jit(solution)/shard_map/ppermute | solution.py:1669
  183.0 13.9 %collective-permute-start.12 = (bf16[2,192,384]{2,1,0:T(8,128)(2,1)S(1)}, bf16[2,192,384]{2,1,0:T(8,128)(2,1)S(1)}, u32[]{:S(2)}, u32[]{:S(2)}) collective-permute-start(bf16[2,192,384]{2,1,0:T(8,128)(2,1)S(1)} %get-tuple-element.182), channel_id=1, source_target_pairs={{0,16},{2,18},{4,20},{6,22},{8,24},{10,26},{12,28},{14,30},{16,0},... | collective-permute-start | bytes 884744 | tf_op jit(solution)/shard_map/ppermute | solution.py:1669
  185.6 12.7 %collective-permute-start.11 = (bf16[4,192,384]{2,1,0:T(8,128)(2,1)S(1)}, bf16[4,192,384]{2,1,0:T(8,128)(2,1)S(1)}, u32[]{:S(2)}, u32[]{:S(2)}) collective-permute-start(bf16[4,192,384]{2,1,0:T(8,128)(2,1)S(1)} %get-tuple-element.180), channel_id=1, source_target_pairs={{0,4},{2,6},{4,0},{6,2},{8,12},{10,14},{12,8},{14,10},{16,20},{18,... | collective-permute-start | bytes 1769480 | tf_op jit(solution)/shard_map/ppermute | solution.py:1669
  194.6 1.3 collective-permute-start.13
  198.4 7.6 %collective-permute-start.14 = (bf16[2,192,384]{2,1,0:T(8,128)(2,1)S(1)}, bf16[2,192,384]{2,1,0:T(8,128)(2,1)S(1)}, u32[]{:S(2)}, u32[]{:S(2)}) collective-permute-start(bf16[2,192,384]{2,1,0:T(8,128)(2,1)S(1)} %get-tuple-element.186), channel_id=1, source_target_pairs={{0,8},{2,10},{4,12},{6,14},{8,0},{10,2},{12,4},{14,6},{16,24},{18,... | collective-permute-start | bytes 884744 | tf_op jit(solution)/shard_map/ppermute | solution.py:1669
  199.0 3.9 %collective-permute-start.15 = (f32[4,8,256]{2,1,0:T(8,128)S(1)}, f32[4,8,256]{2,1,0:T(8,128)S(1)}, u32[]{:S(2)}, u32[]{:S(2)}) collective-permute-start(f32[4,8,256]{2,1,0:T(8,128)S(1)} %get-tuple-element.189), channel_id=1, source_target_pairs={{0,4},{2,6},{4,0},{6,2},{8,12},{10,14},{12,8},{14,10},{16,20},{18,... | collective-permute-start | bytes 98312 | tf_op jit(solution)/shard_map/ppermute | solution.py:1669
  206.1 7.5 %collective-permute-start.16 = (bf16[1,192,384]{2,1,0:T(8,128)(2,1)S(1)}, bf16[1,192,384]{2,1,0:T(8,128)(2,1)S(1)}, u32[]{:S(2)}, u32[]{:S(2)}) collective-permute-start(bf16[1,192,384]{2,1,0:T(8,128)(2,1)S(1)} %get-tuple-element.191), channel_id=1, source_target_pairs={{0,16},{2,18},{4,20},{6,22},{8,24},{10,26},{12,28},{14,30},{16,0},... | collective-permute-start | bytes 442376 | tf_op jit(solution)/shard_map/ppermute | solution.py:1669
  206.6 8.9 %collective-permute-start.20 = (bf16[2,192,384]{2,1,0:T(8,128)(2,1)S(1)}, bf16[2,192,384]{2,1,0:T(8,128)(2,1)S(1)}, u32[]{:S(2)}, u32[]{:S(2)}) collective-permute-start(bf16[2,192,384]{2,1,0:T(8,128)(2,1)S(1)} %get-tuple-element.197.own_ref), channel_id=1, source_target_pairs={{0,1},{1,0},{2,3},{3,2},{4,5},{5,4},{6,7},{7,6},{8,9},{9,8},{10,11... | collective-permute-start | bytes 884744 | tf_op jit(solution)/shard_map/ppermute | solution.py:1788
  207.3 3.8 %collective-permute-start.17 = (f32[2,8,256]{2,1,0:T(8,128)S(1)}, f32[2,8,256]{2,1,0:T(8,128)S(1)}, u32[]{:S(2)}, u32[]{:S(2)}) collective-permute-start(f32[2,8,256]{2,1,0:T(8,128)S(1)} %get-tuple-element.193), channel_id=1, source_target_pairs={{0,8},{2,10},{4,12},{6,14},{8,0},{10,2},{12,4},{14,6},{16,24},{18,... | collective-permute-start | bytes 49160 | tf_op jit(solution)/shard_map/ppermute | solution.py:1669
  213.6 5.2 %collective-permute-start.18 = (bf16[192,384]{1,0:T(8,128)(2,1)S(1)}, bf16[192,384]{1,0:T(8,128)(2,1)S(1)}, u32[]{:S(2)}, u32[]{:S(2)}) collective-permute-start(bf16[192,384]{1,0:T(8,128)(2,1)S(1)} %bitcast.12), channel_id=1, source_target_pairs={{0,1},{1,0},{2,3},{3,2},{4,5},{5,4},{6,7},{7,6},{8,9},{9,8},{10,11... | collective-permute-start | bytes 442376 | tf_op jit(solution)/shard_map/ppermute | solution.py:1788
  214.3 4.5 %collective-permute-start.19 = (f32[1,8,256]{2,1,0:T(8,128)S(1)}, f32[1,8,256]{2,1,0:T(8,128)S(1)}, u32[]{:S(2)}, u32[]{:S(2)}) collective-permute-start(f32[1,8,256]{2,1,0:T(8,128)S(1)} %get-tuple-element.196), channel_id=1, source_target_pairs={{0,16},{2,18},{4,20},{6,22},{8,24},{10,26},{12,28},{14,30},{16,0},... | collective-permute-start | bytes 24584 | tf_op jit(solution)/shard_map/ppermute | solution.py:1669
  (11 other events, 56.5 us)

commit v2 on v1

--- a/solution.py
+++ b/solution.py
@@ -726,7 +726,7 @@
     small = ((8, 128), low)
     scratch = [kept[0], kept[1], kept[2] if train else ((1, 8, 128), low), kept[3], kept[4], kept[5]]
     scratch += [kept[6], kept[7], kept[8]] if train else [small, small, ((8, 128), full)]
-    out_shape = [jax.ShapeDtypeStruct((count, width), low)]
+    out_shape = [pltpu.VMEM((count, width), low)]
     out_specs = [whole_vmem()]
     if train:
         out_shape += [jax.ShapeDtypeStruct(*item) for item in kept]
@@ -802,7 +802,7 @@
     entries = table.shape[0]
     span = TABLE_SPAN
     steps = entries // span
-    rows = pl.BlockSpec((count, width), lambda j: (0, 0))
+    rows = whole_vmem()
     wide = pl.BlockSpec((count, span), lambda j: (0, j))
     return pl.pallas_call(
         logits_kernel,
@@ -825,7 +825,7 @@
             flops=4 * count * width * entries, bytes_accessed=60_000_000, transcendentals=0
         ),
         name="logits_phase",
-    )(student, teacher, *far(table))
+    )(*near(student, teacher), *far(table))
 
 
 def joined_norms(own, other):
@@ -1781,7 +1781,7 @@
         compiler_params=pltpu.CompilerParams(vmem_limit_bytes=16 << 20),
         cost_estimate=pl.CostEstimate(flops=1_000_000, bytes_accessed=1_000_000, transcendentals=0),
         name="finish",
-    )(place, own, other, keep, got, ready)
+    )(place, own, other, keep, got, *far(ready))
 
 
 def swap(value):

time: 224 us -> 221 us (0.987)
    unnamed x28 -> x24, local copies, waits for them, and re-layouts: 6.21 us -> 4.02 us
  transfers between devices with their start and end apart: 21 -> 21, of which waited for: 13 -> 13; matrix products, arithmetic and copies ran while one was open for 0% -> 0% of each run, Pallas kernels for 20% -> 21%
where the time goes in v2:
time: 221 us; the launch traced here: 219 us
  Pallas kernels  156 us (71%)
  waiting for transfers between devices  32.3 us (15%)
  starting transfers between devices  23.9 us (11%)
  local copies, waits for them, and re-layouts  4.58 us (2%)
    pallas_call x2, Pallas kernels, forward(): pl.pallas_call(functools.partial(forward_kernel, train), in_specs=[scalar...  39.6 us
    pallas_call x1, Pallas kernels, logits_phase(): pl.pallas_call(logits_kernel, grid=(steps,), in_specs=[rows, rows, pl.Blo...  39.3 us
    ppermute x15, waiting for transfers between devices, across(): lax.ppermute(value, 'dp', [(i, i ^ mask) for i in range(lax.axis_size('dp...  21.1 us
    pallas_call x1, Pallas kernels, gradient_phase(): pl.pallas_call(functools.partial(gradient_kernel, joint), grid=(steps,),...  20.2 us
    ppermute x15, starting transfers between devices, across(): lax.ppermute(value, 'dp', [(i, i ^ mask) for i in range(lax.axis_size('dp...  14.3 us
    ppermute x6, waiting for transfers between devices, swap(): return lax.ppermute(value, 'blk', [(0, 1), (1, 0)])  11.3 us
    pallas_call x1, Pallas kernels, feed_back(): pl.pallas_call(feed_kernel, grid=(1,), in_specs=[scalars()] + [whole_vmem...  10.3 us
    ppermute x6, starting transfers between devices, swap(): return lax.ppermute(value, 'blk', [(0, 1), (1, 0)])  9.53 us
  transfers between devices with their start and end apart: 21, of which 13 were waited for; matrix products, arithmetic and copies ran while one was open for 0% of the time, Pallas kernels for 21%

profile of v2, /device:TPU:0, one launch (start us, length us, event | category | flops | bytes accessed | tf_op | source)
XLA Modules:
  0.0 218.6 jit_solution(15479731476598507103)
XLA Ops:
  0.6 3.0 %collective-permute-start = (bf16[256,768]{1,0:T(8,128)(2,1)}, bf16[256,768]{1,0:T(8,128)(2,1)S(1)}, u32[]{:S(2)}, u32[]{:S(2)}) collective-permute-start(bf16[256,768]{1,0:T(8,128)(2,1)} %refs_1_.5), channel_id=1, source_target_pairs={{0,1},{1,0},{2,3},{3,2},{4,5},{5,4},{6,7},{7,6},{8,9},{9,8},{10,11... | collective-permute-start | bytes 1179656 | tf_op jit(solution)/shard_map/ppermute | solution.py:1788
  3.8 9.2 %collective-permute-done.refs_3_.refs_2_ = bf16[256,768]{1,0:T(8,128)(2,1)S(1)} collective-permute-done((bf16[256,768]{1,0:T(8,128)(2,1)}, bf16[256,768]{1,0:T(8,128)(2,1)S(1)}, u32[]{:S(2)}, u32[]{:S(2)}) %collective-permute-start) | collective-permute-done | bytes 393248 | tf_op jit(solution)/shard_map/ppermute | solution.py:1788
  14.7 18.2 %forward_teacher.1.teacher_ref = bf16[512,768]{1,0:T(8,128)(2,1)S(1)} custom-call(s32[2]{0:T(128)S(1)} %pad_add_fusion.refs_0_.place_ref, s32[1,4]{1,0:T(1,128)S(1)} %copy-done.8, bf16[256,768]{1,0:T(8,128)(2,1)S(1)} %copy-done.6, bf16[256,768]{1,0:T(8,128)(2,1)S(1)} %collective-permute-done.refs_3_.refs_2_, f32[768]{0:T(1024)} %refs_4_.4, f32[768]{0:T(1024)} %refs_5_.3, ...), custom_call_target="tpu_custom_call" | custom-call | flops 8000000000 | bytes 20000000 | tf_op jit(solution)/shard_map/forward_teacher/pallas_call | solution.py:734
  32.9 21.4 %forward_student.1 = (bf16[512,768]{1,0:T(8,128)(2,1)S(1)}, bf16[512,768]{1,0:T(8,128)(2,1)}, bf16[512,2304]{1,0:T(8,128)(2,1)}, bf16[12,512,512]{2,1,0:T(8,128)...) custom-call(s32[2]{0:T(128)} %copy-done, ...), custom_call_target="tpu_custom_call" | custom-call | flops 8000000000 | bytes 20000000 | tf_op jit(solution)/shard_map/forward_student/pallas_call | solution.py:734
  54.3 39.3 %logits_phase.1 = (bf16[512,16384]{1,0:T(8,128)(2,1)S(1)}, bf16[512,16384]{1,0:T(8,128)(2,1)}, f32[8,40,512]{2,1,0:T(8,128)S(1)}, f32[8,512]{1,0:T(8,128)S(1)}) custom-call(bf16[512,768]{1,0:T(8,128)(2,1)S(1)} %get-tuple-element.112.student_ref, bf16[512,768]{1,0:T(8,128)(2,1)S(1)} %forward_teacher.1.teacher_ref, bf16[16384,768]{1,0:T(8,128)(2,1)} %table_ref.5), custom_call_target="tpu_custom_call" | custom-call | flops 25769803776 | bytes 60000000 | tf_op jit(solution)/shard_map/logits_phase/pallas_call | solution.py:807
  93.6 1.7 collective-permute-start.1
  95.4 2.0 collective-permute-done.1.other_ref
  97.4 20.2 %gradient_phase.1 = (f32[256,768]{1,0:T(8,128)S(1)}, bf16[256,768]{1,0:T(8,128)(2,1)S(1)}, f32[256,768]{1,0:T(8,128)S(1)}, f32[8,512]{1,0:T(8,128)S(1)}, bf16[768,3072]{1,0:T(8,128)(2,1)S(1)}) custom-call(bf16[512,16384]{1,0:T(8,128)(2,1)S(1)} %get-tuple-element.113.diff_first.diff_second.diff_ref, ...), custom_call_target="tpu_custom_call" | custom-call | flops 12884901888 | bytes 60000000 | tf_op jit(solution)/shard_map/gradient_phase/pallas_call | solution.py:950
  117.6 1.8 collective-permute-start.2
  119.4 9.3 %gradient_rest.1 = (f32[256,768]{1,0:T(8,128)S(1)}, bf16[256,768]{1,0:T(8,128)(2,1)S(1)}) custom-call(bf16[512,16384]{1,0:T(8,128)(2,1)S(1)} %get-tuple-element.113.diff_first.diff_second.diff_ref, bf16[512,16384]{1,0:T(8,128)(2,1)} %get-tuple-element.114.expo_first.expo_second.expo_ref, bf16[16384,768]{1,0:T(8,128)(2,1)} %table_ref.5, ...), custom_call_target="tpu_custom_call" | custom-call | flops 12000000000 | bytes 1000000 | tf_op jit(solution)/shard_map/gradient_rest/pallas_call | solution.py:1014
  130.4 2.3 %copy-done.2 = bf16[3072,768]{1,0:T(8,128)(2,1)S(1)} copy-done((bf16[3072,768]{1,0:T(8,128)(2,1)S(1)}, bf16[3072,768]{1,0:T(8,128)(2,1)}, u32[]{:S(2)}) %copy-start.2) | copy-done | bytes 4718616
  132.7 5.8 %first_rows.1 = (bf16[256,768]{1,0:T(8,128)(2,1)S(1)}, bf16[256,3072]{1,0:T(8,128)(2,1)S(1)}, f32[256,768]{1,0:T(8,128)S(1)}, bf16[256,768]{1,0:T(8,128)(2,1)S(1...) custom-call(f32[256,768]{1,0:T(8,128)S(1)} %get-tuple-element.120.ow, ...), custom_call_target="tpu_custom_call" | custom-call | flops 12000000000 | bytes 1000000 | tf_op jit(solution)/shard_map/first_rows/pallas_call | solution.py:1137
  138.6 10.3 %feed_back.1 = (bf16[8,192,384]{2,1,0:T(8,128)(2,1)S(1)}, bf16[8,192,384]{2,1,0:T(8,128)(2,1)S(1)}, bf16[8,192,384]{2,1,0:T(8,128)(2,1)S(1)}, bf16[8,192,384]{2,...) custom-call(s32[2]{0:T(128)S(1)} %copy-done.1, ...), custom_call_target="tpu_custom_call" | custom-call | flops 12000000000 | bytes 1000000 | tf_op jit(solution)/shard_map/feed_back/pallas_call | solution.py:1252
  149.5 4.9 %branch_back.1 = (f32[256,768]{1,0:T(8,128)S(1)}, bf16[256,768]{1,0:T(8,128)(2,1)S(1)}, bf16[16,48,384]{2,1,0:T(8,128)(2,1)S(1)}, f32[1,768]{1,0:T(1,128)S(1)}, ...) custom-call(s32[2]{0:T(128)S(1)} %copy-done.1, ...), custom_call_target="tpu_custom_call", output_to_operand_aliasing={{6}: (12, {}), {7}: (13, {})} | custom-call | flops 12000000000 | bytes 1000000 | tf_op jit(solution)/shard_map/branch_back/pallas_call | solution.py:1340
  157.9 8.5 %project_back.1 = (bf16[512,384]{1,0:T(8,128)(2,1)S(1)}, bf16[512,384]{1,0:T(8,128)(2,1)S(1)}, bf16[512,384]{1,0:T(8,128)(2,1)S(1)}, bf16[8,192,384]{2,1,0:T(8,1...) custom-call(s32[2]{0:T(128)S(1)} %copy-done.1, ...), custom_call_target="tpu_custom_call", output_to_operand_aliasing={{5}: (9, {}), {6}: (10, {})} | custom-call | flops 12000000000 | bytes 1000000 | tf_op jit(solution)/shard_map/project_back/pallas_call | solution.py:1540
  166.5 3.4 %collective-permute-done.6.refs_1_ = bf16[4,192,384]{2,1,0:T(8,128)(2,1)S(1)} collective-permute-done((bf16[4,192,384]{2,1,0:T(8,128)(2,1)S(1)}, bf16[4,192,384]{2,1,0:T(8,128)(2,1)S(1)}, u32[]{:S(2)}, u32[]{:S(2)}) %collective-permute-start.6) | collective-permute-done | bytes 589856 | tf_op jit(solution)/shard_map/ppermute | solution.py:1669
  173.7 6.3 %attend_back.1 = (bf16[512,384]{1,0:T(8,128)(2,1)S(1)}, bf16[512,384]{1,0:T(8,128)(2,1)S(1)}, bf16[512,384]{1,0:T(8,128)(2,1)S(1)}, bf16[8,192,384]{2,1,0:T(8,12...) custom-call(s32[2]{0:T(128)S(1)} %copy-done.1, ...), custom_call_target="tpu_custom_call", output_to_operand_aliasing={{3}: (7, {}), {4}: (8, {}), {5}: (9, {})} | custom-call | flops 12000000000 | bytes 1000000 | tf_op jit(solution)/shard_map/attend_back/pallas_call | solution.py:1511
  181.0 2.6 %collective-permute-start.12 = (bf16[2,192,384]{2,1,0:T(8,128)(2,1)S(1)}, bf16[2,192,384]{2,1,0:T(8,128)(2,1)S(1)}, u32[]{:S(2)}, u32[]{:S(2)}) collective-permute-start(bf16[2,192,384]{2,1,0:T(8,128)(2,1)S(1)} %get-tuple-element.182), channel_id=1, source_target_pairs={{0,16},{2,18},{4,20},{6,22},{8,24},{10,26},{12,28},{14,30},{16,0},... | collective-permute-start | bytes 884744 | tf_op jit(solution)/shard_map/ppermute | solution.py:1669
  184.4 8.2 %input_back.1 = (f32[256,768]{1,0:T(8,128)}, f32[8,8,256]{2,1,0:T(8,128)S(1)}, f32[8,8,256]{2,1,0:T(8,128)S(1)}, bf16[4,192,384]{2,1,0:T(8,128)(2,1)S(1)}, bf16[2,192,384]{2,1,0:T(8,128)(2,1)S(1)}) custom-call(s32[2]{0:T(128)S(1)} %copy-done.1, bf16[256,768]{1,0:T(8,128)(2,1)} %refs_1_.5, ...), custom_call_target="tpu_custom_call", output_to_operand_aliasing={{3}: (18, {}), {4}: (19, {})} | custom-call | flops 12000000000 | bytes 1000000 | tf_op jit(solution)/shard_map/input_back/pallas_call | solution.py:1645
  198.4 2.6 %collective-permute-done.15.refs_5_ = f32[4,8,256]{2,1,0:T(8,128)S(1)} collective-permute-done((f32[4,8,256]{2,1,0:T(8,128)S(1)}, f32[4,8,256]{2,1,0:T(8,128)S(1)}, u32[]{:S(2)}, u32[]{:S(2)}) %collective-permute-start.15) | collective-permute-done | bytes 32800 | tf_op jit(solution)/shard_map/ppermute | solution.py:1669
  201.0 3.1 %collective-permute-done.14.refs_1_ = bf16[2,192,384]{2,1,0:T(8,128)(2,1)S(1)} collective-permute-done((bf16[2,192,384]{2,1,0:T(8,128)(2,1)S(1)}, bf16[2,192,384]{2,1,0:T(8,128)(2,1)S(1)}, u32[]{:S(2)}, u32[]{:S(2)}) %collective-permute-start.14) | collective-permute-done | bytes 294944 | tf_op jit(solution)/shard_map/ppermute | solution.py:1669
  205.3 1.7 collective-permute-start.17
  207.0 2.0 collective-permute-done.17.refs_3_
  209.1 2.5 %collective-permute-done.16.refs_1_ = bf16[1,192,384]{2,1,0:T(8,128)(2,1)S(1)} collective-permute-done((bf16[1,192,384]{2,1,0:T(8,128)(2,1)S(1)}, bf16[1,192,384]{2,1,0:T(8,128)(2,1)S(1)}, u32[]{:S(2)}, u32[]{:S(2)}) %collective-permute-start.16) | collective-permute-done | bytes 147488 | tf_op jit(solution)/shard_map/ppermute | solution.py:1669
  (65 shorter events, 26.7 us)
Async XLA Ops:
  0.6 12.4 %collective-permute-start = (bf16[256,768]{1,0:T(8,128)(2,1)}, bf16[256,768]{1,0:T(8,128)(2,1)S(1)}, u32[]{:S(2)}, u32[]{:S(2)}) collective-permute-start(bf16[256,768]{1,0:T(8,128)(2,1)} %refs_1_.5), channel_id=1, source_target_pairs={{0,1},{1,0},{2,3},{3,2},{4,5},{5,4},{6,7},{7,6},{8,9},{9,8},{10,11... | collective-permute-start | bytes 1179656 | tf_op jit(solution)/shard_map/ppermute | solution.py:1788
  3.8 29.1 %copy-start = (s32[2]{0:T(128)}, s32[2]{0:T(128)S(1)}, u32[]{:S(2)}) copy-start(s32[2]{0:T(128)S(1)} %pad_add_fusion.refs_0_.place_ref) | copy-start | bytes 28
  14.7 18.2 %copy-start.7 = (bf16[256,768]{1,0:T(8,128)(2,1)}, bf16[256,768]{1,0:T(8,128)(2,1)S(1)}, u32[]{:S(2)}) copy-start(bf16[256,768]{1,0:T(8,128)(2,1)S(1)} %collective-permute-done.refs_3_.refs_2_) | copy-start | bytes 1179652
  93.6 3.7 %collective-permute-start.1 = (f32[8,512]{1,0:T(8,128)S(1)}, f32[8,512]{1,0:T(8,128)S(1)}, u32[]{:S(2)}, u32[]{:S(2)}) collective-permute-start(f32[8,512]{1,0:T(8,128)S(1)} %get-tuple-element.116.own_ref), channel_id=1, source_target_pairs={{0,1},{1,0},{2,3},{3,2},{4,5},{5,4},{6,7},{7,6},{8,9},{9,8},{10,11... | collective-permute-start | bytes 49160 | tf_op jit(solution)/shard_map/ppermute | solution.py:1788
  117.6 12.8 %copy-start.3 = (bf16[768,3072]{1,0:T(8,128)(2,1)}, bf16[768,3072]{1,0:T(8,128)(2,1)S(1)}, u32[]{:S(2)}) copy-start(bf16[768,3072]{1,0:T(8,128)(2,1)S(1)} %get-tuple-element.124.we.refs_10_) | copy-start | bytes 14155780
  117.6 12.7 %collective-permute-start.2 = (bf16[256,768]{1,0:T(8,128)(2,1)S(1)}, bf16[256,768]{1,0:T(8,128)(2,1)S(1)}, u32[]{:S(2)}, u32[]{:S(2)}) collective-permute-start(bf16[256,768]{1,0:T(8,128)(2,1)S(1)} %get-tuple-element.121), channel_id=1, source_target_pairs={{0,1},{1,0},{2,3},{3,2},{4,5},{5,4},{6,7},{7,6},{8,9},{9,8},{10,11... | collective-permute-start | bytes 1179656 | tf_op jit(solution)/shard_map/ppermute | solution.py:1788
  128.8 9.8 %collective-permute-start.3 = (bf16[256,768]{1,0:T(8,128)(2,1)S(1)}, bf16[256,768]{1,0:T(8,128)(2,1)S(1)}, u32[]{:S(2)}, u32[]{:S(2)}) collective-permute-start(bf16[256,768]{1,0:T(8,128)(2,1)S(1)} %get-tuple-element.129), channel_id=1, source_target_pairs={{0,1},{1,0},{2,3},{3,2},{4,5},{5,4},{6,7},{7,6},{8,9},{9,8},{10,11... | collective-permute-start | bytes 1179656 | tf_op jit(solution)/shard_map/ppermute | solution.py:1788
  148.9 5.5 %collective-permute-start.4 = (bf16[8,192,384]{2,1,0:T(8,128)(2,1)S(1)}, bf16[8,192,384]{2,1,0:T(8,128)(2,1)S(1)}, u32[]{:S(2)}, u32[]{:S(2)}) collective-permute-start(bf16[8,192,384]{2,1,0:T(8,128)(2,1)S(1)} %get-tuple-element.149), channel_id=1, source_target_pairs={{0,2},{2,0},{4,6},{6,4},{8,10},{10,8},{12,14},{14,12},{16,18},{18,... | collective-permute-start | bytes 3538952 | tf_op jit(solution)/shard_map/ppermute | solution.py:1669
  149.0 7.1 %collective-permute-start.5 = (bf16[8,192,384]{2,1,0:T(8,128)(2,1)S(1)}, bf16[8,192,384]{2,1,0:T(8,128)(2,1)S(1)}, u32[]{:S(2)}, u32[]{:S(2)}) collective-permute-start(bf16[8,192,384]{2,1,0:T(8,128)(2,1)S(1)} %get-tuple-element.151), channel_id=1, source_target_pairs={{0,2},{2,0},{4,6},{6,4},{8,10},{10,8},{12,14},{14,12},{16,18},{18,... | collective-permute-start | bytes 3538952 | tf_op jit(solution)/shard_map/ppermute | solution.py:1669
  154.5 15.4 %collective-permute-start.6 = (bf16[4,192,384]{2,1,0:T(8,128)(2,1)S(1)}, bf16[4,192,384]{2,1,0:T(8,128)(2,1)S(1)}, u32[]{:S(2)}, u32[]{:S(2)}) collective-permute-start(bf16[4,192,384]{2,1,0:T(8,128)(2,1)S(1)} %get-tuple-element.212), channel_id=1, source_target_pairs={{0,4},{2,6},{4,0},{6,2},{8,12},{10,14},{12,8},{14,10},{16,20},{18,... | collective-permute-start | bytes 1769480 | tf_op jit(solution)/shard_map/ppermute | solution.py:1669
  156.2 15.1 %collective-permute-start.7 = (bf16[4,192,384]{2,1,0:T(8,128)(2,1)S(1)}, bf16[4,192,384]{2,1,0:T(8,128)(2,1)S(1)}, u32[]{:S(2)}, u32[]{:S(2)}) collective-permute-start(bf16[4,192,384]{2,1,0:T(8,128)(2,1)S(1)} %get-tuple-element.210), channel_id=1, source_target_pairs={{0,8},{2,10},{4,12},{6,14},{8,0},{10,2},{12,4},{14,6},{16,24},{18,... | collective-permute-start | bytes 1769480 | tf_op jit(solution)/shard_map/ppermute | solution.py:1669
  166.4 14.3 %collective-permute-start.8 = (bf16[8,192,384]{2,1,0:T(8,128)(2,1)S(1)}, bf16[8,192,384]{2,1,0:T(8,128)(2,1)S(1)}, u32[]{:S(2)}, u32[]{:S(2)}) collective-permute-start(bf16[8,192,384]{2,1,0:T(8,128)(2,1)S(1)} %get-tuple-element.171), channel_id=1, source_target_pairs={{0,2},{2,0},{4,6},{6,4},{8,10},{10,8},{12,14},{14,12},{16,18},{18,... | collective-permute-start | bytes 3538952 | tf_op jit(solution)/shard_map/ppermute | solution.py:1669
  171.5 8.5 %collective-permute-start.9 = (bf16[2,192,384]{2,1,0:T(8,128)(2,1)S(1)}, bf16[2,192,384]{2,1,0:T(8,128)(2,1)S(1)}, u32[]{:S(2)}, u32[]{:S(2)}) collective-permute-start(bf16[2,192,384]{2,1,0:T(8,128)(2,1)S(1)} %get-tuple-element.173), channel_id=1, source_target_pairs={{0,8},{2,10},{4,12},{6,14},{8,0},{10,2},{12,4},{14,6},{16,24},{18,... | collective-permute-start | bytes 884744 | tf_op jit(solution)/shard_map/ppermute | solution.py:1669
  173.1 7.6 %collective-permute-start.10 = (bf16[2,192,384]{2,1,0:T(8,128)(2,1)S(1)}, bf16[2,192,384]{2,1,0:T(8,128)(2,1)S(1)}, u32[]{:S(2)}, u32[]{:S(2)}) collective-permute-start(bf16[2,192,384]{2,1,0:T(8,128)(2,1)S(1)} %get-tuple-element.175), channel_id=1, source_target_pairs={{0,4},{2,6},{4,0},{6,2},{8,12},{10,14},{12,8},{14,10},{16,20},{18,... | collective-permute-start | bytes 884744 | tf_op jit(solution)/shard_map/ppermute | solution.py:1669
  181.0 13.9 %collective-permute-start.12 = (bf16[2,192,384]{2,1,0:T(8,128)(2,1)S(1)}, bf16[2,192,384]{2,1,0:T(8,128)(2,1)S(1)}, u32[]{:S(2)}, u32[]{:S(2)}) collective-permute-start(bf16[2,192,384]{2,1,0:T(8,128)(2,1)S(1)} %get-tuple-element.182), channel_id=1, source_target_pairs={{0,16},{2,18},{4,20},{6,22},{8,24},{10,26},{12,28},{14,30},{16,0},... | collective-permute-start | bytes 884744 | tf_op jit(solution)/shard_map/ppermute | solution.py:1669
  183.6 12.7 %collective-permute-start.11 = (bf16[4,192,384]{2,1,0:T(8,128)(2,1)S(1)}, bf16[4,192,384]{2,1,0:T(8,128)(2,1)S(1)}, u32[]{:S(2)}, u32[]{:S(2)}) collective-permute-start(bf16[4,192,384]{2,1,0:T(8,128)(2,1)S(1)} %get-tuple-element.180), channel_id=1, source_target_pairs={{0,4},{2,6},{4,0},{6,2},{8,12},{10,14},{12,8},{14,10},{16,20},{18,... | collective-permute-start | bytes 1769480 | tf_op jit(solution)/shard_map/ppermute | solution.py:1669
  192.6 1.3 collective-permute-start.13
  196.4 7.6 %collective-permute-start.14 = (bf16[2,192,384]{2,1,0:T(8,128)(2,1)S(1)}, bf16[2,192,384]{2,1,0:T(8,128)(2,1)S(1)}, u32[]{:S(2)}, u32[]{:S(2)}) collective-permute-start(bf16[2,192,384]{2,1,0:T(8,128)(2,1)S(1)} %get-tuple-element.186), channel_id=1, source_target_pairs={{0,8},{2,10},{4,12},{6,14},{8,0},{10,2},{12,4},{14,6},{16,24},{18,... | collective-permute-start | bytes 884744 | tf_op jit(solution)/shard_map/ppermute | solution.py:1669
  197.0 3.9 %collective-permute-start.15 = (f32[4,8,256]{2,1,0:T(8,128)S(1)}, f32[4,8,256]{2,1,0:T(8,128)S(1)}, u32[]{:S(2)}, u32[]{:S(2)}) collective-permute-start(f32[4,8,256]{2,1,0:T(8,128)S(1)} %get-tuple-element.189), channel_id=1, source_target_pairs={{0,4},{2,6},{4,0},{6,2},{8,12},{10,14},{12,8},{14,10},{16,20},{18,... | collective-permute-start | bytes 98312 | tf_op jit(solution)/shard_map/ppermute | solution.py:1669
  204.1 7.5 %collective-permute-start.16 = (bf16[1,192,384]{2,1,0:T(8,128)(2,1)S(1)}, bf16[1,192,384]{2,1,0:T(8,128)(2,1)S(1)}, u32[]{:S(2)}, u32[]{:S(2)}) collective-permute-start(bf16[1,192,384]{2,1,0:T(8,128)(2,1)S(1)} %get-tuple-element.191), channel_id=1, source_target_pairs={{0,16},{2,18},{4,20},{6,22},{8,24},{10,26},{12,28},{14,30},{16,0},... | collective-permute-start | bytes 442376 | tf_op jit(solution)/shard_map/ppermute | solution.py:1669
  204.6 8.9 %collective-permute-start.20 = (bf16[2,192,384]{2,1,0:T(8,128)(2,1)S(1)}, bf16[2,192,384]{2,1,0:T(8,128)(2,1)S(1)}, u32[]{:S(2)}, u32[]{:S(2)}) collective-permute-start(bf16[2,192,384]{2,1,0:T(8,128)(2,1)S(1)} %get-tuple-element.197.own_ref), channel_id=1, source_target_pairs={{0,1},{1,0},{2,3},{3,2},{4,5},{5,4},{6,7},{7,6},{8,9},{9,8},{10,11... | collective-permute-start | bytes 884744 | tf_op jit(solution)/shard_map/ppermute | solution.py:1788
  205.3 3.8 %collective-permute-start.17 = (f32[2,8,256]{2,1,0:T(8,128)S(1)}, f32[2,8,256]{2,1,0:T(8,128)S(1)}, u32[]{:S(2)}, u32[]{:S(2)}) collective-permute-start(f32[2,8,256]{2,1,0:T(8,128)S(1)} %get-tuple-element.193), channel_id=1, source_target_pairs={{0,8},{2,10},{4,12},{6,14},{8,0},{10,2},{12,4},{14,6},{16,24},{18,... | collective-permute-start | bytes 49160 | tf_op jit(solution)/shard_map/ppermute | solution.py:1669
  211.6 5.2 %collective-permute-start.18 = (bf16[192,384]{1,0:T(8,128)(2,1)S(1)}, bf16[192,384]{1,0:T(8,128)(2,1)S(1)}, u32[]{:S(2)}, u32[]{:S(2)}) collective-permute-start(bf16[192,384]{1,0:T(8,128)(2,1)S(1)} %bitcast.12), channel_id=1, source_target_pairs={{0,1},{1,0},{2,3},{3,2},{4,5},{5,4},{6,7},{7,6},{8,9},{9,8},{10,11... | collective-permute-start | bytes 442376 | tf_op jit(solution)/shard_map/ppermute | solution.py:1788
  212.3 4.5 %collective-permute-start.19 = (f32[1,8,256]{2,1,0:T(8,128)S(1)}, f32[1,8,256]{2,1,0:T(8,128)S(1)}, u32[]{:S(2)}, u32[]{:S(2)}) collective-permute-start(f32[1,8,256]{2,1,0:T(8,128)S(1)} %get-tuple-element.196), channel_id=1, source_target_pairs={{0,16},{2,18},{4,20},{6,22},{8,24},{10,26},{12,28},{14,30},{16,0},... | collective-permute-start | bytes 24584 | tf_op jit(solution)/shard_map/ppermute | solution.py:1669
  (9 other events, 54.3 us)
